TPU v7x, 32 devices: a whole 2x2x4 slice. The times are simulated.
32 devices in a mesh: var: 4 (over y, x), item: 8 (over z, core).
Axes of the slice: x: 2, y: 2, z: 4, core: 2. Of those that a mesh axis runs over, the one named last changes fastest.
Arguments:
- fields: bfloat16 [8, 12, 4, 2048], P('item', 'var'), may hold values from -6 to 6
- var_mask: int32 [8, 12], P('item'), may hold values from 0 to 1, as said below
- embed_weight: bfloat16 [12, 4, 1024], P('var'), may hold values from -3 to 3
- var_embed: bfloat16 [12, 1024], P('var'), may hold values from -6 to 6
- agg_query: bfloat16 [1024], replicated, may hold values from -6 to 6
- agg_key: bfloat16 [1024, 1024], replicated, may hold values from -0.1875 to 0.1875
- agg_value: bfloat16 [1024, 1024], replicated, may hold values from -0.1875 to 0.1875
- agg_out: bfloat16 [1024, 1024], replicated, may hold values from -0.375 to 0.375
- norm1_gain: float32 [1024], replicated, may hold values from 0.25 to 1.75
- norm1_bias: float32 [1024], replicated, may hold values from -3 to 3
- attn_qkv: bfloat16 [1024, 3072], replicated, may hold values from -0.1875 to 0.1875
- attn_proj: bfloat16 [1024, 1024], replicated, may hold values from -0.75 to 0.75
- norm2_gain: float32 [1024], replicated, may hold values from 0.25 to 1.75
- norm2_bias: float32 [1024], replicated, may hold values from -3 to 3
- mlp_in: bfloat16 [1024, 4096], replicated, may hold values from -0.1875 to 0.1875
- mlp_out: bfloat16 [4096, 1024], replicated, may hold values from -0.09375 to 0.09375
- cotangent: bfloat16 [8, 2048, 1024], P('item', 'var'), may hold values from -6 to 6
Outputs:
- output: bfloat16 [8, 2048, 1024], P('item', 'var')
- fields_grad: float32 [8, 12, 4, 2048], P('item', 'var')
- embed_weight_grad: float32 [12, 4, 1024], P('var', None, 'item')
- var_embed_grad: float32 [12, 1024], P('var', 'item')
- agg_query_grad: float32 [1024], P('item')
- agg_key_grad: float32 [1024, 1024], P('item')
- agg_value_grad: float32 [1024, 1024], P('item')
- agg_out_grad: float32 [1024, 1024], P('item')
- norm1_gain_grad: float32 [1024], P('item')
- norm1_bias_grad: float32 [1024], P('item')
- attn_qkv_grad: float32 [1024, 3072], P('item')
- attn_proj_grad: float32 [1024, 1024], P('item')
- norm2_gain_grad: float32 [1024], P('item')
- norm2_bias_grad: float32 [1024], P('item')
- mlp_in_grad: float32 [1024, 4096], P('item')
- mlp_out_grad: float32 [4096, 1024], P('item')
Inputs may be any that keep to these rules, and one draw needn't show every extreme that they name: `var_mask`: in every item at least 7 of the 12 slots are 1; which ones differs from item to item.
All inputs are finite; a program needn't handle non-finite values.
Results may differ from a plain program's by a relative error of at most 0.018.
Values may be sent and summed in bfloat16 or wider, within the bound.
No kernel may reach another device: no remote copies, remote signals or barrier semaphores. Data moves between devices by JAX's collectives and lax.ppermute only.
A program may use at most 448 MiB of HBM per device.

v0:
```python
from functools import partial

import jax
import jax.numpy as jnp
from jax import lax
from jax.experimental import pallas as pl
from jax.experimental.pallas import tpu as pltpu
from jax.sharding import Mesh
from jax.sharding import PartitionSpec as P

HEADS = 16
TABLES = 5

epsilon = 1e-05
masked_score = -1e30
highest = lax.Precision.HIGHEST
f32 = jnp.float32
bf16 = jnp.bfloat16
COST = 0.05
VMEM_BYTES = 56 * 1024 * 1024
LOG2E = 1.4426950408889634


def dot(a, b):
    return lax.dot_general(a, b, (((1,), (0,)), ((), ())), preferred_element_type=f32)


def dot_nt(a, b):
    return lax.dot_general(a, b, (((1,), (1,)), ((), ())), preferred_element_type=f32)


def dot_tn(a, b):
    return lax.dot_general(a, b, (((0,), (0,)), ((), ())), preferred_element_type=f32)


def split_two(wide):
    high = wide.astype(bf16)
    return high, (wide - high.astype(f32)).astype(bf16)


def split_three(wide):
    high, rest = split_two(wide)
    low = wide - high.astype(f32) - rest.astype(f32)
    return high, rest, low.astype(bf16)


def columns(parts, rows, width):
    lane = lax.broadcasted_iota(jnp.int32, (rows, width), 1)
    out = jnp.zeros((rows, width), f32)
    for i, part in enumerate(parts):
        out = jnp.where(lane == i, part.astype(f32), out)
    return out.astype(bf16)


def whole(shape):
    return pl.BlockSpec(shape, lambda *_: (0,) * len(shape))


def params(vmem=VMEM_BYTES):
    return pltpu.CompilerParams(vmem_limit_bytes=vmem)


def cost(flops, bytes_accessed, transcendentals=0, share=COST):
    return pl.CostEstimate(
        flops=int(flops * share), bytes_accessed=int(bytes_accessed * share), transcendentals=0
    )


def norm_parts(stream):
    centred = stream - jnp.mean(stream, axis=-1, keepdims=True)
    inverse = lax.rsqrt(jnp.mean(centred * centred, axis=-1, keepdims=True) + epsilon)
    return centred * inverse, inverse


def norm_back(upstream, unit_rows, inverse, gain):
    scaled = upstream * gain
    return inverse * (
        scaled
        - jnp.mean(scaled, axis=-1, keepdims=True)
        - unit_rows * jnp.mean(scaled * unit_rows, axis=-1, keepdims=True)
    )


def variable_probs(pixel_rows, score_high, score_low, real, slots):
    scores = dot(score_high, pixel_rows) + dot(score_low, pixel_rows)
    scores = scores.reshape(HEADS, slots, pixel_rows.shape[1])
    scores = jnp.where(real[None] > 0, scores, masked_score)
    powers = jnp.exp(scores - jnp.max(scores, axis=1, keepdims=True))
    return powers / jnp.sum(powers, axis=1, keepdims=True)


def prep_kernel(count, vars_here, patches, *refs):
    place_ref = refs[0]
    pieces = refs[1 : 1 + count]
    query_ref, key_ref, value_ref = refs[1 + count : 4 + count]
    (
        pix_ref, tables_ref, shi_ref, slo_ref, sthi_ref, stlo_ref, front_ref, back_ref, keys_ref,
        qk_ref, spread_ref, all_s,
    ) = refs[4 + count :]
    me = place_ref[0]
    depth, width = tables_ref.shape
    slots = depth // TABLES
    size = width // HEADS
    rows = TABLES * vars_here
    total = None
    for d in range(count):
        row = lax.broadcasted_iota(jnp.int32, (depth, rows), 0)
        col = lax.broadcasted_iota(jnp.int32, (depth, rows), 1)
        want = (col % TABLES) * slots + (me ^ d) * vars_here + col // TABLES
        part = dot(jnp.where(row == want, 1.0, 0.0).astype(bf16), pieces[d][...])
        total = part if total is None else total + part
    all_s[...] = total.astype(bf16)
    mine = patches // count
    for d in range(count):
        at = pl.multiple_of((me ^ d) * mine, mine)
        pix_ref[:, d * mine : (d + 1) * mine] = all_s[:, pl.ds(at, mine)]
    tables = all_s[:, patches:]
    tables_ref[...] = tables
    head = lax.broadcasted_iota(jnp.int32, (HEADS, width), 0)
    same = lax.broadcasted_iota(jnp.int32, (HEADS, width), 1) // size == head
    spread = jnp.where(same, query_ref[...].astype(f32), 0.0)
    scale = size ** (-0.5)
    spread_ref[...] = (spread * scale).astype(bf16)
    query_keys = (dot_nt(key_ref[...], spread.astype(bf16)) * scale).astype(bf16)
    qk_ref[...] = query_keys
    halves = split_two(dot(tables, query_keys))
    wide = HEADS * slots
    picks = lax.broadcasted_iota(jnp.int32, (wide, HEADS), 0) // slots
    picks = jnp.where(picks == lax.broadcasted_iota(jnp.int32, (wide, HEADS), 1), 1.0, 0.0).astype(bf16)
    for half, tall, flat in zip(halves, (shi_ref, slo_ref), (sthi_ref, stlo_ref)):
        row = lax.broadcasted_iota(jnp.int32, (wide, depth), 0) % slots
        col = lax.broadcasted_iota(jnp.int32, (wide, depth), 1) % slots
        tall[...] = jnp.where(row == col, dot_nt(picks, half), 0.0).astype(bf16)
        row = lax.broadcasted_iota(jnp.int32, (depth, wide), 0) % slots
        col = lax.broadcasted_iota(jnp.int32, (depth, wide), 1) % slots
        flat[...] = jnp.where(row == col, dot_nt(half, picks), 0.0).astype(bf16)
    mixed = dot(tables, value_ref[...])
    high, low = split_two(mixed)
    high_wide, low_wide = high.astype(f32), low.astype(f32)
    front_ref[...] = jnp.concatenate([high_wide, high_wide, low_wide], axis=0).T.astype(bf16)
    both = jnp.concatenate([high, low], axis=0)
    for h in range(HEADS):
        back_ref[h] = both[:, h * size : (h + 1) * size]
    keys_ref[...] = dot(tables, key_ref[...])


def front_kernel(
    own_blocks, n_z, place_ref, pix_ref, shi_ref, slo_ref, real_ref, ev_ref, out_w_ref, gain_ref,
    bias_ref, wq_ref, wk_ref, wv_ref,
    values_ref, merged_ref, send_ref, keep_ref, q_ref, k_ref, v_ref, flat_ref, tall_s,
):
    slots = real_ref.shape[0]
    pixel_rows = pix_ref[...]
    probs = variable_probs(pixel_rows, shi_ref[...], slo_ref[...], real_ref[...], slots)
    weights = probs.astype(bf16).astype(f32)
    pixels = pixel_rows.astype(f32).reshape(TABLES, slots, -1)
    size = ev_ref.shape[0] // HEADS
    for h in range(HEADS):
        mixed = (weights[h][None] * pixels).reshape(pixel_rows.shape)
        high, low = split_two(mixed)
        flat_ref[h * size : (h + 1) * size, :] = dot(
            ev_ref[h * size : (h + 1) * size, :], jnp.concatenate([high, low, high], axis=0)
        )
    values = flat_ref[...].astype(bf16)
    merged = dot(values.T, out_w_ref[...])

    @pl.when(pl.program_id(0) < own_blocks)
    def _():
        values_ref[...] = values
        merged_ref[...] = merged

    unit_rows, _ = norm_parts(merged)
    normed = (unit_rows * gain_ref[...] + bias_ref[...]).astype(bf16)
    tall_s[...] = normed.T
    core, shard = place_ref[1], tall_s.shape[0] // (2 * n_z)
    for zz in range(n_z):
        at = slice(zz * shard, (zz + 1) * shard)
        keep_ref[at] = tall_s[pl.ds(pl.multiple_of((2 * zz + core) * shard, shard), shard), :]
        send_ref[at] = tall_s[pl.ds(pl.multiple_of((2 * zz + 1 - core) * shard, shard), shard), :]
    queries = dot(normed, wq_ref[...]).astype(bf16).astype(f32) * size ** (-0.5)
    keys = dot(normed, wk_ref[...])
    values = dot(normed, wv_ref[...])
    for h in range(q_ref.shape[0]):
        at = h * size
        q_ref[h] = queries[:, at : at + size].astype(bf16)
        k_ref[h] = keys[:, at : at + size].astype(bf16)
        v_ref[h] = values[:, at : at + size].astype(bf16)


def attend_kernel(q_ref, k_ref, v_ref, out_ref, lse_ref):
    here, rows, size = q_ref.shape
    block = min(512, rows)
    pieces = [(h, at) for at in range(0, rows, block) for h in range(here)]

    def scores_of(piece):
        h, at = piece
        return dot_nt(q_ref[h, at : at + block], k_ref[h])

    def finish(piece, powers, top, total):
        h, at = piece
        mixed = dot(powers, v_ref[h]) / total
        lse = jnp.broadcast_to(top + jnp.log(total), (block, 128)).T[0:1]
        return mixed.astype(bf16), lse

    done, waiting = {}, None
    scores = scores_of(pieces[0])
    for i, piece in enumerate(pieces):
        later = scores_of(pieces[i + 1]) if i + 1 < len(pieces) else None
        top = jnp.max(scores, axis=-1, keepdims=True)
        powers = jnp.exp(scores - top)
        total = jnp.sum(powers, axis=-1, keepdims=True)
        if waiting is not None:
            done[waiting[0]] = finish(*waiting)
        waiting = (piece, powers.astype(bf16), top, total)
        scores = later
    done[waiting[0]] = finish(*waiting)
    for h, at in pieces:
        lse_ref[h, :, at : at + block] = done[h, at][1]
    for at in range(0, rows, block):
        out_ref[at : at + block] = jnp.concatenate([done[h, at][0] for h in range(here)], axis=-1)


def attend_back_kernel(count, extra, *refs):
    extra_refs, refs = refs[:extra], refs[extra:]
    q_ref, k_ref, v_ref = refs[:3]
    lse_refs = refs[3 : 3 + count]
    out_refs = refs[3 + count : 3 + 2 * count]
    up_refs = refs[3 + 2 * count : 3 + 3 * count]
    full_ref = refs[3 + 3 * count]
    piece_refs = refs[4 + 3 * count : 4 + 4 * count]
    up_heads, total_rows, lse_rows, gq_ref, prob_s, slope_s = refs[4 + 4 * count :]
    step = pl.program_id(0)
    here, patches, size = q_ref.shape
    block = k_ref.shape[1]
    width = here * size
    mine = patches // count

    @pl.when(step == 0)
    def _():
        for h in range(here):
            at = h * size
            for d in range(count):
                rows = slice(d * mine, (d + 1) * mine)
                upstream = up_refs[d][:, at : at + size]
                up_heads[h, rows] = upstream
                product = upstream.astype(f32) * out_refs[d][:, at : at + size].astype(f32)
                total_rows[h, :, rows] = jnp.sum(product.T, axis=0, keepdims=True)
                lse_rows[h, :, rows] = lse_refs[d][h]
            gq_ref[h] = jnp.zeros(gq_ref.shape[1:], f32)

    chunk = min(256, patches)
    key_parts, value_parts = [], []
    for h in range(here):
        keys, values = k_ref[h], v_ref[h]
        for at in range(0, patches, chunk):
            span = slice(at, at + chunk)
            probs = jnp.exp(dot_nt(keys, q_ref[h, span]) - lse_rows[h, :, span])
            prob_s[h, :, span] = probs.astype(bf16)
            grads = dot_nt(values, up_heads[h, span])
            slope_s[h, :, span] = (probs * (grads - total_rows[h, :, span])).astype(bf16)
        value_parts.append(dot(prob_s[h], up_heads[h]))
        key_parts.append(dot(slope_s[h], q_ref[h]))
        gq_ref[h] += dot(keys.astype(f32).T.astype(bf16), slope_s[h])
    rows = pl.ds(pl.multiple_of(step * block, block), block)
    full_ref[rows, width : 2 * width] = jnp.concatenate(key_parts, axis=-1).astype(bf16)
    full_ref[rows, 2 * width :] = jnp.concatenate(value_parts, axis=-1).astype(bf16)

    @pl.when(step == pl.num_programs(0) - 1)
    def _():
        scale = size ** (-0.5)
        query_parts = [gq_ref[h].T for h in range(here)]
        full_ref[:, :width] = (jnp.concatenate(query_parts, axis=-1) * scale).astype(bf16)
        for d in range(count):
            piece_refs[d][:, : 3 * width] = full_ref[d * mine : (d + 1) * mine, :]

    if extra:

        @pl.when(step == 0)
        def _():
            for d in range(count):
                piece_refs[d][:, 3 * width :] = extra_refs[d][...]


def mlp_kernel(pieces, count, *refs):
    place_ref = refs[0]
    att_refs = refs[1 : 1 + pieces]
    merged_ref, proj_ref, gain_ref, bias_ref, cot_ref, win_ref, wout_ref = refs[1 + pieces : 8 + pieces]
    outs = refs[8 + pieces :]
    (
        out_ref, att_t_ref, normed_t_ref, send_ref, keep_ref, ghid_ref, gstream_ref, glow_ref,
        gains_ref,
    ) = outs[:9]
    gatt_refs = outs[9 : 9 + count]
    att_s, normed_s, stream_s, unit_s, inv_s, out_s, gn_s, tall_s = outs[9 + count :]
    step = pl.program_id(0)
    me = place_ref[0]
    cols = gatt_refs[0].shape[1]

    @pl.when(step == 0)
    def _():
        if pieces == 1:
            attended = att_refs[0][...]
        else:
            for d in range(pieces):
                att_s[:, pl.ds(pl.multiple_of((me ^ d) * cols, cols), cols)] = att_refs[d][...]
            attended = att_s[...]
        att_t_ref[...] = attended.T
        stream = merged_ref[...] + dot(attended, proj_ref[...])
        unit_rows, inverse = norm_parts(stream)
        stream_s[...] = stream
        unit_s[...] = unit_rows
        inv_s[...] = inverse
        normed = (unit_rows * gain_ref[...] + bias_ref[...]).astype(bf16)
        normed_s[...] = normed
        normed_t_ref[...] = normed.T
        out_s[...] = jnp.zeros_like(out_s)
        gn_s[...] = jnp.zeros_like(gn_s)

    tile = ghid_ref.shape[1]
    sub = min(256, tile)
    spans = [slice(at, at + sub) for at in range(0, tile, sub)]
    normed_rows, upstream_rows = normed_s[...], cot_ref[...]

    def products(span):
        return dot(normed_rows, win_ref[:, span]), dot_nt(upstream_rows, wout_ref[span, :])

    def shape(hidden, g_active):
        below = 0.5 + 0.5 * lax.erf(hidden * (0.5**0.5))
        density = jnp.exp(-0.5 * hidden * hidden) * ((2.0 * jnp.pi) ** (-0.5))
        return (hidden * below).astype(bf16), (g_active * (below + hidden * density)).astype(bf16)

    actives, grads, sums = [], [], []

    def add(first, last):
        span = slice(spans[first].start, spans[last].stop)
        active = jnp.concatenate(actives[first : last + 1], axis=1)
        grad = jnp.concatenate(grads[first : last + 1], axis=1)
        sums.append((dot(active, wout_ref[span, :]), dot_nt(grad, win_ref[:, span])))

    ready = products(spans[0])
    for i, span in enumerate(spans):
        later = products(spans[i + 1]) if i + 1 < len(spans) else None
        if i == len(spans) // 2 + 1:
            add(0, len(spans) // 2 - 1)
        active, grad = shape(*ready)
        actives.append(active)
        grads.append(grad)
        ready = later
    add(len(spans) // 2 if sums else 0, len(spans) - 1)
    for span, active, grad in zip(spans, actives, grads):
        ghid_ref[:, span] = grad
        tall_s[span, :] = active.T
    half = tile // 2
    core = place_ref[1]
    send_ref[...] = tall_s[pl.ds(pl.multiple_of((1 - core) * half, half), half), :]
    keep_ref[...] = tall_s[pl.ds(pl.multiple_of(core * half, half), half), :]
    out_s[...] += sum(pair[0] for pair in sums)
    gn_s[...] += sum(pair[1] for pair in sums)

    @pl.when(step == pl.num_programs(0) - 1)
    def _():
        out_ref[...] = (stream_s[...] + out_s[...]).astype(bf16)
        upstream = gn_s[...].astype(bf16).astype(f32)
        unit_rows = unit_s[...]
        g_stream = cot_ref[...].astype(f32) + norm_back(
            upstream, unit_rows, inv_s[...], gain_ref[...]
        )
        gstream_ref[...] = g_stream
        low = g_stream.astype(bf16)
        glow_ref[...] = low
        for d in range(count):
            rows = pl.ds(pl.multiple_of((me ^ d) * cols, cols), cols)
            gatt_refs[d][...] = dot_nt(low, proj_ref[rows, :]).astype(bf16)
        gains_ref[0:1, :] = jnp.sum(upstream * unit_rows, axis=0, keepdims=True)
        gains_ref[1:2, :] = jnp.sum(upstream, axis=0, keepdims=True)


def send_kernel(place_ref, main_rows, main_cols, side_rows, side_cols, out_ref):
    last = pl.program_id(0) == pl.num_programs(0) - 1

    def product(rows_ref, cols_ref):
        tall = rows_ref[...].reshape(-1, rows_ref.shape[-1])
        return dot(tall, cols_ref[...]).astype(bf16)

    @pl.when(jnp.logical_not(last))
    def _():
        out_ref[...] = product(main_rows, main_cols)

    @pl.when(last)
    def _():
        out_ref[...] = product(side_rows, side_cols)


def keep_kernel(count, *refs):
    main_rows, main_cols, main_got, side_rows, side_cols, side_got = refs[1:7]
    outs = refs[7:]
    step = pl.program_id(0)

    def product(rows_ref, cols_ref, got_ref):
        tall = rows_ref[...].reshape(-1, rows_ref.shape[-1])
        return (dot(tall, cols_ref[...]) + got_ref[...].astype(f32)).astype(bf16)

    for d in range(count):

        @pl.when(step == d)
        def _():
            first, second = outs[d], outs[count + d]
            main = product(main_rows, main_cols, main_got)
            cut = first.shape[1]
            rest = main.shape[1] - cut
            first[...] = main[:, :cut]
            second[:, :rest] = main[:, cut:]
            second[:, rest:] = product(side_rows, side_cols, side_got)


def pair_kernel(count, channels, vars_here, late_rows, *refs):
    place_ref = refs[0]
    keep_ref, got_ref, n_keep_ref, n_got_ref, fields_ref = refs[1:6]
    outs = refs[6:]
    depth, mine = fields_ref.shape
    rows = late_rows
    span = outs[0].shape[1]
    slots = depth // TABLES
    n_blocks = n_keep_ref.shape[1] // span
    f_rows = (outs[0].shape[0] - rows - n_blocks * HEADS) // (mine // span)
    row = lax.broadcasted_iota(jnp.int32, (f_rows, depth), 0)
    col = lax.broadcasted_iota(jnp.int32, (f_rows, depth), 1)
    n_total = (n_keep_ref[...] + n_got_ref[...].astype(f32)).astype(bf16)
    for d in range(count):
        q = place_ref[0] ^ d

        def block(ref):
            if len(ref.shape) == 3:
                return ref[d, :rows].astype(f32)
            return ref[:rows, pl.ds(pl.multiple_of(q * span, span), span)].astype(f32)

        outs[d][:rows] = (block(keep_ref) + block(got_ref)).astype(bf16)
        want = (row % channels) * slots + q * vars_here + row // channels
        picks = jnp.where((want == col) & (row < channels * vars_here), 1.0, 0.0).astype(bf16)
        picked = dot(picks, fields_ref[...]).astype(bf16)
        at = rows
        for b in range(n_blocks):
            outs[d][at : at + HEADS] = n_total[:, b * span : (b + 1) * span]
            at += HEADS
        for b in range(mine // span):
            outs[d][at : at + f_rows] = picked[:, b * span : (b + 1) * span]
            at += f_rows


def z_pieces_kernel(count, shard, n_z, *refs):
    pieces, outs, fields_ref, total_s = refs[1 : 1 + count], refs[1 + count : -2], refs[-2], refs[-1]
    me, z_at = refs[0][0], refs[0][2]
    rows, span = total_s.shape
    f_rows = fields_ref.shape[0]
    mine = fields_ref.shape[1] // count
    total = pieces[0][:rows].astype(f32)
    for piece in pieces[1:]:
        total = total + piece[:rows].astype(f32)
    total_s[...] = total.astype(bf16)
    for d in range(n_z):
        start = pl.multiple_of((z_at ^ d) * shard, shard)
        outs[d][:shard] = total_s[pl.ds(start, shard), :]
        outs[d][shard:] = total_s[n_z * shard :, :]
    for d in range(count):
        blocks = [
            pieces[d][rows + b * f_rows : rows + (b + 1) * f_rows] for b in range(mine // span)
        ]
        at = pl.multiple_of((me ^ d) * mine, mine)
        fields_ref[:, pl.ds(at, mine)] = jnp.concatenate(blocks, axis=1).astype(f32)


def assemble_kernel(count, parts, size, halves, *refs):
    me = refs[0][0]
    blocks, outs = refs[1 : 1 + count + halves], refs[1 + count + halves :]
    in_ref, proj_ref, qkv_ref, out_ref = outs
    a = in_ref.shape[1] // count
    b = proj_ref.shape[1] // count
    width = proj_ref.shape[1]
    for d in range(count):
        if halves and d == count - 1:
            rows = jnp.concatenate([ref[...] for ref in blocks[d:]], axis=1)
        else:
            rows = blocks[d][...]
        rows = rows.astype(f32)
        q = me ^ d if halves else d

        def span(at, step):
            return pl.ds(pl.multiple_of(at, step) if halves else at, step)

        in_ref[:, span(q * a, a)] = rows[:, :a]
        proj_ref[:, span(q * b, b)] = rows[:, a : a + b]
        at = a + b
        for part in range(parts):
            for third in range(3):
                to = third * width + q * b + part * size
                qkv_ref[:, span(to, size)] = rows[:, at : at + size]
                at += size
        out_ref[q] = rows[:, at:]


def z_sum_kernel(count, *refs):
    pieces, (rows_ref, n_ref) = refs[:count], refs[count:]
    total = pieces[0][...].astype(f32)
    for piece in pieces[1:]:
        total = total + piece[...].astype(f32)
    rows, span = rows_ref.shape
    rows_ref[...] = total[:rows].astype(bf16)
    for b in range(n_ref.shape[1] // span):
        n_ref[:, b * span : (b + 1) * span] = total[rows + b * HEADS : rows + (b + 1) * HEADS]


def final_kernel(count, *refs):
    place_ref = refs[0]
    pieces = refs[1 : 1 + count]
    n_ref, tables_ref, spread_ref, keys_ref, value_ref, qk_ref = refs[1 + count : 7 + count]
    outg_ref, valg_ref, keyg_ref, queryg_ref, embedg_ref, varg_ref, gains_ref, m_s = refs[7 + count :]
    shard, depth = tables_ref.shape
    width = m_s.shape[1]
    for d in range(count):
        span = pieces[d].shape[1]
        at = 0 if count == 1 else pl.multiple_of((place_ref[0] ^ d) * span, span)
        outg_ref[:, pl.ds(at, span)] = pieces[d][:shard].astype(f32)
        m_s[:, pl.ds(at, span)] = pieces[d][shard:].astype(f32)
    m_low = m_s[:depth, :].astype(bf16)
    n_high, n_low = split_two(n_ref[:, :depth])
    tables = tables_ref[...]
    valg_ref[...] = dot(tables, m_low)
    g_qk = dot_nt(tables, n_high) + dot_nt(tables, n_low)
    qk_high, qk_low = split_two(g_qk)
    spread = spread_ref[...]
    keyg_ref[...] = dot(qk_high, spread) + dot(qk_low, spread)
    head_at = lax.broadcasted_iota(jnp.int32, (HEADS, width), 1) // (width // HEADS)
    same = head_at == lax.broadcasted_iota(jnp.int32, (HEADS, width), 0)
    ones = jnp.where(same, 1.0, 0.0).astype(bf16)
    n_wide = dot(n_high.astype(f32).T.astype(bf16), ones) + dot(n_low.astype(f32).T.astype(bf16), ones)
    queryg_ref[...] = jnp.sum(n_wide * keys_ref[...], axis=0, keepdims=True)
    qk = qk_ref[...]
    table_grad = split_three(
        dot_nt(m_low, value_ref[...])
        + dot_nt(n_high.astype(f32).T.astype(bf16), qk)
        + dot_nt(n_low.astype(f32).T.astype(bf16), qk)
    )
    slots = depth // TABLES
    vars_here = varg_ref.shape[0]
    for ref, first, each in ((embedg_ref, 0, TABLES - 1), (varg_ref, TABLES - 1, 1)):
        row = lax.broadcasted_iota(jnp.int32, (each * vars_here, depth), 0)
        col = lax.broadcasted_iota(jnp.int32, (each * vars_here, depth), 1)
        want = (first + row % each) * slots + place_ref[0] * vars_here + row // each
        picks = jnp.where(want == col, 1.0, 0.0).astype(bf16)
        ref[...] = sum(dot(picks, part) for part in table_grad)
    gains_ref[...] = m_s[depth : depth + 8, :]


def back_kernel(count, parts, n_z, *refs):
    place_ref = refs[0]
    piece_refs = refs[1 : 1 + count * parts]
    (
        qkv_far, merged_far, gain_ref, gs_far, out_w_far, pix_ref, shi_ref, slo_ref, sthi_ref,
        stlo_ref, real_ref, ev_ref, values_far, gains_two_ref,
        fields_ref, send_ref, keep_ref, slope_s, packed_s, m_ref, n_ref,
        qkv_s, merged_ref, gs_ref, out_w_ref, values_ref, copied,
    ) = refs[1 + count * parts :]
    width = merged_ref.shape[1]
    thirds = [
        pltpu.make_async_copy(
            qkv_far.at[:, pl.ds(third * width, width)], qkv_s.at[third], copied.at[third]
        )
        for third in range(3)
    ]
    others = [
        pltpu.make_async_copy(far, near, copied.at[3 + i])
        for i, (far, near) in enumerate(
            [
                (merged_far, merged_ref), (gs_far, gs_ref), (out_w_far, out_w_ref),
                (values_far, values_ref),
            ]
        )
    ]
    for copy in thirds + others:
        copy.start()
    slots = real_ref.shape[0]
    if count == 1:
        packed = piece_refs[0][...]
    else:
        span = piece_refs[0].shape[1] // 3
        for third in range(3):
            for part in range(parts):
                for d in range(count):
                    at = third * (count * parts) + (place_ref[0] ^ d) * parts + part
                    packed_s[:, pl.ds(pl.multiple_of(at * span, span), span)] = piece_refs[
                        part * count + d
                    ][:, third * span : (third + 1) * span]
        packed = packed_s[...]
    pixel_rows = pix_ref[...]
    probs = variable_probs(pixel_rows, shi_ref[...], slo_ref[...], real_ref[...], slots)
    weights = probs.astype(bf16).astype(f32)
    pixels = pixel_rows.astype(f32).reshape(TABLES, slots, -1)
    upstream = None
    for third, copy in enumerate(thirds):
        copy.wait()
        product = dot_nt(packed[:, third * width : (third + 1) * width], qkv_s[third])
        upstream = product if upstream is None else upstream + product
    upstream = upstream.astype(bf16).astype(f32)
    for copy in others:
        copy.wait()
    unit_rows, inverse = norm_parts(merged_ref[...])
    g_merged = gs_ref[...] + norm_back(upstream, unit_rows, inverse, gain_ref[...])
    low = g_merged.astype(bf16)
    depth = pix_ref.shape[0]
    m_ref[...] = jnp.zeros_like(m_ref)
    m_ref[depth + 2 : depth + 4, :] = gains_two_ref[...]
    m_ref[depth : depth + 1, :] = jnp.sum(upstream * unit_rows, axis=0, keepdims=True)
    m_ref[depth + 1 : depth + 2, :] = jnp.sum(upstream, axis=0, keepdims=True)
    g_values = dot_nt(low, out_w_ref[...]).astype(bf16)
    grads = dot(values_ref[...], low)
    size = ev_ref.shape[2]
    g_fields = jnp.zeros(pixels.shape, f32)
    for h in range(HEADS):
        rows = g_values[:, h * size : (h + 1) * size]
        both = dot_nt(ev_ref[h], rows)
        table = (both[:depth] + both[depth:]).reshape(pixels.shape)
        g_weights = jnp.sum(pixels * table, axis=0)
        total = jnp.sum(g_weights * probs[h], axis=0, keepdims=True)
        slope_s[h * slots : (h + 1) * slots, :] = (probs[h] * (g_weights - total)).astype(bf16)
        g_fields += weights[h][None] * table
        mixed = (weights[h][None] * pixels).reshape(pixel_rows.shape)
        pair = dot(jnp.concatenate(split_two(mixed), axis=0), rows)
        m_ref[:depth, h * size : (h + 1) * size] = pair[:depth] + pair[depth:]
    slopes = slope_s[...]
    fields_ref[...] = (
        g_fields.reshape(pixel_rows.shape) + dot(sthi_ref[...], slopes) + dot(stlo_ref[...], slopes)
    ).astype(bf16)
    n_ref[...] = dot_nt(pixel_rows, slopes)

    core = place_ref[1]
    shard = grads.shape[0] // (2 * n_z)
    for zz in range(n_z):
        at = slice(zz * shard, (zz + 1) * shard)
        even = grads[2 * zz * shard : (2 * zz + 1) * shard]
        odd = grads[(2 * zz + 1) * shard : (2 * zz + 2) * shard]
        keep_ref[at] = jnp.where(core == 0, even, odd)
        send_ref[at] = jnp.where(core == 0, odd, even).astype(bf16)
    top = n_z * shard
    middle = top + m_ref.shape[0]
    tables = m_ref[...]
    keep_ref[top:middle] = tables
    send_ref[top:middle] = tables.astype(bf16)
    columns = lax.broadcasted_iota(jnp.int32, n_ref.shape, 1)
    same = columns % slots == lax.broadcasted_iota(jnp.int32, n_ref.shape, 0) % slots
    n_high, n_low = split_two(jnp.where(same, n_ref[...], 0.0))
    heads = (HEADS, n_ref.shape[1])
    picks = lax.broadcasted_iota(jnp.int32, heads, 1) // slots
    picks = jnp.where(picks == lax.broadcasted_iota(jnp.int32, heads, 0), 1.0, 0.0).astype(bf16)
    n_rows = dot_nt(picks, n_high) + dot_nt(picks, n_low)
    keep_ref[middle:] = jnp.zeros((HEADS, keep_ref.shape[1]), f32)
    keep_ref[middle:, :depth] = n_rows
    send_ref[middle:] = keep_ref[middle:].astype(bf16)


def per_device(
    n_var, n_z, fields, var_mask, embed_weight, var_embed, agg_query, agg_key, agg_value, agg_out,
    norm1_gain, norm1_bias, attn_qkv, attn_proj, norm2_gain, norm2_bias, mlp_in, mlp_out, cotangent,
):
    n_item = 2 * n_z
    width = agg_key.shape[0]
    size = width // HEADS
    scale = size ** (-0.5)
    hidden_width = mlp_in.shape[1]
    vars_here, channels, patches = fields.shape[1:]
    slot_count = var_mask.shape[1]
    slots = -(-slot_count // 16) * 16
    mine = patches // n_var
    here = HEADS // n_var
    cols = here * size
    shard = width // n_item
    me = lax.axis_index("var")
    core = lax.axis_index("core")
    z_at = lax.axis_index("z")
    item = z_at * 2 + core
    rel = me ^ jnp.arange(n_var)
    rel_z = z_at ^ jnp.arange(n_z)
    place = jnp.stack([me, core, z_at]).astype(jnp.int32)
    lanes_fit = cols % 128 == 0

    def send(array, other):
        return lax.ppermute(array, "var", [(i, i ^ other) for i in range(n_var)])

    def send_z(array, other):
        return lax.ppermute(array, "z", [(i, i ^ other) for i in range(n_z)])

    def swap_core(array):
        return lax.ppermute(array, "core", [(0, 1), (1, 0)])

    def canonical(by_distance):
        return jnp.take(jnp.stack(by_distance, axis=0), rel, axis=0)

    def call(kernel, grid, in_specs, out_specs, out_shape, scratch, estimate, name, *args):
        return pl.pallas_call(
            kernel,
            grid_spec=pltpu.PrefetchScalarGridSpec(
                num_scalar_prefetch=1,
                grid=grid,
                in_specs=in_specs,
                out_specs=out_specs,
                scratch_shapes=scratch,
            ),
            out_shape=out_shape,
            compiler_params=params(),
            cost_estimate=estimate,
            name=name,
        )(place, *args)

    depth = TABLES * slots
    pixel_part = jnp.concatenate([fields[0], jnp.ones((vars_here, 1, patches), bf16)], axis=1)
    table_part = jnp.concatenate([embed_weight, var_embed[:, None, :]], axis=1)
    piece = jnp.concatenate([pixel_part, table_part], axis=2).reshape(TABLES * vars_here, -1)
    pieces = [piece] + [send(piece, d) for d in range(1, n_var)]
    real = jnp.pad(var_mask[0], (0, slots - slot_count)).astype(f32)[:, None]
    prep_in = pieces + [agg_query[None], agg_key, agg_value]
    maps = [(HEADS * slots, depth)] * 2 + [(depth, HEADS * slots)] * 2
    prep_out = (
        [((depth, patches), bf16), ((depth, width), bf16)]
        + [(shape, bf16) for shape in maps]
        + [
            ((width, 3 * depth), bf16),
            ((HEADS, 2 * depth, size), bf16),
            ((depth, width), f32),
            ((width, HEADS), bf16),
            ((HEADS, width), bf16),
        ]
    )
    (
        pixels, tables, score_high, score_low, score_high_t, score_low_t, ev_front, ev_back,
        table_keys, query_keys, spread,
    ) = call(
        partial(prep_kernel, n_var, vars_here, patches),
        (1,),
        [whole(array.shape) for array in prep_in],
        [whole(shape) for shape, _ in prep_out],
        [jax.ShapeDtypeStruct(shape, kind) for shape, kind in prep_out],
        [pltpu.VMEM((depth, patches + width), bf16)],
        cost(8 * depth * width * width, 4 * width * width),
        "prep",
        *prep_in,
    )

    gain_one, bias_one = norm1_gain[None], norm1_bias[None]
    gain_two, bias_two = norm2_gain[None], norm2_bias[None]

    if lanes_fit:
        qkv_parts = [attn_qkv] * 3
        qkv_specs = [
            pl.BlockSpec((width, cols), lambda i, at, third=third: (0, third * n_var + at[0]))
            for third in range(3)
        ]
    else:
        qkv_mine = lax.dynamic_index_in_dim(
            attn_qkv.reshape(width, 3, n_var, cols), me, axis=2, keepdims=False
        )
        qkv_parts = [qkv_mine[:, third] for third in range(3)]
        qkv_specs = [whole((width, cols))] * 3

    block = min(512, mine)
    steps = patches // block
    own = mine // block
    heads_shape = jax.ShapeDtypeStruct((here, patches, size), bf16)
    heads_spec = pl.BlockSpec((here, block, size), lambda i, _: (0, i, 0))
    agg_values_t, merged, normed_send, normed_keep, queries, keys, values = call(
        partial(front_kernel, own, n_z),
        (steps,),
        [
            pl.BlockSpec((depth, block), lambda i, _: (0, i)),
            whole(score_high.shape),
            whole(score_low.shape),
            whole(real.shape),
            whole(ev_front.shape),
            whole(agg_out.shape),
            whole(gain_one.shape),
            whole(bias_one.shape),
        ]
        + qkv_specs,
        [
            pl.BlockSpec((width, block), lambda i, _: (0, jnp.minimum(i, own - 1))),
            pl.BlockSpec((block, width), lambda i, _: (jnp.minimum(i, own - 1), 0)),
            pl.BlockSpec((width // 2, block), lambda i, _: (0, i)),
            pl.BlockSpec((width // 2, block), lambda i, _: (0, i)),
            heads_spec,
            heads_spec,
            heads_spec,
        ],
        [
            jax.ShapeDtypeStruct((width, mine), bf16),
            jax.ShapeDtypeStruct((mine, width), f32),
            jax.ShapeDtypeStruct((width // 2, patches), bf16),
            jax.ShapeDtypeStruct((width // 2, patches), bf16),
            heads_shape,
            heads_shape,
            heads_shape,
        ],
        [pltpu.VMEM((width, block), f32), pltpu.VMEM((width, block), bf16)],
        cost(2 * patches * width * (width + 3 * cols + 256), 16 * patches * width),
        "front",
        pixels, score_high, score_low, real, ev_front, agg_out, gain_one, bias_one, *qkv_parts,
    )

    def attend(distance):
        heads = here
        return pl.pallas_call(
            attend_kernel,
            grid=(here // heads,),
            in_specs=[
                pl.BlockSpec((heads, mine, size), lambda i: (i, distance, 0)),
                pl.BlockSpec((heads, patches, size), lambda i: (i, 0, 0)),
                pl.BlockSpec((heads, patches, size), lambda i: (i, 0, 0)),
            ],
            out_specs=[
                pl.BlockSpec((mine, heads * size), lambda i: (0, i)),
                pl.BlockSpec((heads, 1, mine), lambda i: (i, 0, 0)),
            ],
            out_shape=[
                jax.ShapeDtypeStruct((mine, cols), bf16),
                jax.ShapeDtypeStruct((here, 1, mine), f32),
            ],
            compiler_params=params(),
            cost_estimate=cost(
                4 * mine * patches * here * 256, 4 * patches * cols * 2, mine * patches * here
            ),
            name=f"attend{distance}",
        )(queries, keys, values)

    attended_by, lse_by, arrived = [None] * n_var, [None] * n_var, [None] * n_var
    for distance in reversed(range(n_var)):
        attended_by[distance], lse_by[distance] = attend(distance)
        arrived[distance] = (
            send(attended_by[distance], distance) if distance else attended_by[distance]
        )
    if not lanes_fit:
        arrived = [canonical(arrived).transpose(1, 0, 2).reshape(mine, width)]

    cot = cotangent[0]
    tile = 2 * hidden_width // n_item
    row_f32 = jax.ShapeDtypeStruct((mine, width), f32)
    row_bf16 = jax.ShapeDtypeStruct((mine, width), bf16)
    row_spec = whole((mine, width))
    tall_spec = whole((width, mine))
    tall_bf16 = jax.ShapeDtypeStruct((width, mine), bf16)
    piece_spec = whole((mine, cols))
    (
        output, attended_t, normed_two_t, active_send, active_keep, g_hidden, g_stream, g_stream_low,
        gains_two,
        *g_attended,
    ) = call(
        partial(mlp_kernel, len(arrived), n_var),
        (hidden_width // tile,),
        [whole(piece.shape) for piece in arrived]
        + [
            row_spec,
            whole((width, width)),
            whole(gain_two.shape),
            whole(bias_two.shape),
            row_spec,
            pl.BlockSpec((width, tile), lambda i, _: (0, i)),
            pl.BlockSpec((tile, width), lambda i, _: (i, 0)),
        ],
        [
            row_spec,
            tall_spec,
            tall_spec,
            pl.BlockSpec((tile // 2, mine), lambda i, _: (i, 0)),
            pl.BlockSpec((tile // 2, mine), lambda i, _: (i, 0)),
            pl.BlockSpec((mine, tile), lambda i, _: (0, i)),
            row_spec,
            row_spec,
            whole((2, width)),
        ]
        + [piece_spec] * n_var,
        [
            row_bf16,
            tall_bf16,
            tall_bf16,
            jax.ShapeDtypeStruct((hidden_width // 2, mine), bf16),
            jax.ShapeDtypeStruct((hidden_width // 2, mine), bf16),
            jax.ShapeDtypeStruct((mine, hidden_width), bf16),
            row_f32,
            row_bf16,
            jax.ShapeDtypeStruct((2, width), f32),
        ]
        + [jax.ShapeDtypeStruct((mine, cols), bf16)] * n_var,
        [
            pltpu.VMEM((mine, width), bf16),
            pltpu.VMEM((mine, width), bf16),
            pltpu.VMEM((mine, width), f32),
            pltpu.VMEM((mine, width), f32),
            pltpu.VMEM((mine, 1), f32),
            pltpu.VMEM((mine, width), f32),
            pltpu.VMEM((mine, width), f32),
            pltpu.VMEM((tile, mine), bf16),
        ],
        cost(
            2 * mine * width * (4 * hidden_width + 2 * width),
            4 * width * hidden_width + 16 * mine * width,
        ),
        "mlp",
        *arrived, merged, attn_proj, gain_two, bias_two, cot, mlp_in, mlp_out,
    )
    g_heads = [g_attended[0]] + [send(g_attended[d], d) for d in range(1, n_var)]

    kept_rows = n_z * shard

    def pair_product(tall, grads):
        return dot(tall, grads).astype(bf16)

    def pair_own(tall, grads, got):
        return (dot(tall, grads) + got.astype(f32)).astype(bf16)

    def column_block(array, start=0, total=None):
        rows = array.shape[0]
        total = total or array.shape[1]
        span = total // n_var
        if span % 128 == 0:
            return array, pl.BlockSpec((rows, span), lambda j, at: (0, start // span + (at[0] ^ j)))
        cut = array[:, start : start + total]
        cut = jnp.take(cut.reshape(rows, n_var, span).transpose(1, 0, 2), rel, axis=0)
        return cut, pl.BlockSpec((None, rows, span), lambda j, at: (j, 0, 0))

    def pair_send_two(main, side):
        spec = pl.BlockSpec((n_z, None, shard, mine), lambda j, at: (0, 1 - at[1], 0, 0))
        tiles = hidden_width // width
        return call(
                send_kernel,
                (tiles + 1,),
                [
                    spec,
                    pl.BlockSpec((mine, width), lambda j, at: (0, jnp.minimum(j, tiles - 1))),
                    spec,
                    whole((mine, width)),
                ],
                pl.BlockSpec((kept_rows, width), lambda j, at: (0, j)),
                jax.ShapeDtypeStruct((kept_rows, hidden_width + width), bf16),
                [],
                cost(2 * kept_rows * mine * (hidden_width + width), 24 * kept_rows * width, share=2),
                "send",
                main[0].reshape(n_z, 2, shard, mine), main[1],
                side[0].reshape(n_z, 2, shard, mine), side[1],
            )

    def pair_keep(main, side, got):
        args, specs, start = [], [], 0
        for tall, grads in (main, side):
            args.append(tall.reshape(n_z, 2, shard, mine))
            specs.append(pl.BlockSpec((n_z, None, shard, mine), lambda j, at: (0, at[1], 0, 0)))
            for array, spec in (column_block(grads), column_block(got, start, grads.shape[1])):
                args.append(array)
                specs.append(spec)
            start += grads.shape[1]
        main_span, side_span = main[1].shape[1] // n_var, side[1].shape[1] // n_var
        first = 3 * main_span // 4
        spans = [first] * n_var + [main_span - first + side_span] * n_var
        outs = call(
            partial(keep_kernel, n_var),
            (n_var,),
            specs,
            [whole((kept_rows, span)) for span in spans],
            [jax.ShapeDtypeStruct((kept_rows, span), bf16) for span in spans],
            [],
            cost(
                2 * kept_rows * mine * (main_span + side_span) * n_var, 24 * kept_rows * main_span, share=2
            ),
            "keep",
            *args,
        )
        return outs[:n_var], outs[n_var:]

    def add_all(first, *others):
        total = first.astype(f32)
        for other in others:
            total = total + other.astype(f32)
        return total.astype(bf16)

    def exchange(pieces):
        return [pieces[0]] + [send(pieces[d], d) for d in range(1, n_var)]


    main, side = (normed_two_t, g_hidden), (attended_t, g_stream_low)
    sent = pair_send_two(main, side)
    sent, g_heads, active_send = lax.optimization_barrier((sent, g_heads, active_send))
    got = swap_core(sent)
    got_mlp_out = swap_core(pair_product(active_send, cot))
    first, second = pair_keep(main, side, got)
    active_keep, first, second = lax.optimization_barrier((active_keep, first, second))
    first = exchange(first)
    g_mlp_out = pair_own(active_keep, cot, got_mlp_out)
    mlp_out_rows = lax.psum_scatter(g_mlp_out, "z", scatter_dimension=0, tiled=True)
    g_heads, _ = lax.optimization_barrier((g_heads, g_mlp_out))

    group = min(2, here)
    parts = here // group
    gcols = group * size
    back_block = min(1024, patches)

    def attend_back(part, queries, extra):
        group_spec = pl.BlockSpec((group, back_block, size), lambda i: (part, i, 0))
        side_spec = pl.BlockSpec((mine, gcols), lambda i: (0, part))
        piece_cols = 3 * gcols + sum(array.shape[1] for array in extra[:1])
        full, *pieces = pl.pallas_call(
            partial(attend_back_kernel, n_var, len(extra)),
            grid=(patches // back_block,),
            in_specs=[whole(array.shape) for array in extra]
            + [
                pl.BlockSpec((group, patches, size), lambda i: (part, 0, 0)),
                group_spec,
                group_spec,
            ]
            + [pl.BlockSpec((group, 1, mine), lambda i: (part, 0, 0))] * n_var
            + [side_spec] * (2 * n_var),
            out_specs=[whole((patches, 3 * gcols))] + [whole((mine, piece_cols))] * n_var,
            out_shape=[jax.ShapeDtypeStruct((patches, 3 * gcols), bf16)]
            + [jax.ShapeDtypeStruct((mine, piece_cols), bf16)] * n_var,
            scratch_shapes=[
                pltpu.VMEM((group, patches, size), bf16),
                pltpu.VMEM((group, 1, patches), f32),
                pltpu.VMEM((group, 1, patches), f32),
                pltpu.VMEM((group, size, patches), f32),
                pltpu.VMEM((group, back_block, patches), bf16),
                pltpu.VMEM((group, back_block, patches), bf16),
            ],
            compiler_params=params(),
            cost_estimate=cost(
                10 * patches * patches * group * 256, 8 * patches * gcols * 2, patches * patches * group
            ),
            name=f"attend_back{part}",
        )(*extra, queries, keys, values, *lse_by, *attended_by, *g_heads)
        return full, pieces

    ride = kept_rows == mine and parts > 1
    g_qkv, packed_pieces = [], []
    for part in range(parts):
        full, pieces = attend_back(part, queries, second if ride and part == 0 else [])
        if part == 0:
            full, first = lax.optimization_barrier((full, first))
            first_sum = add_all(*first)
        if part < parts - 1:
            product = pair_product(normed_send, full)
            queries, first_sum, product = lax.optimization_barrier((queries, first_sum, product))
            g_qkv.append((full, product))
        if part == parts - 1:
            pieces, packed_pieces = lax.optimization_barrier((pieces, packed_pieces))
        packed_pieces += exchange(pieces)
    if ride:
        second = [piece[:, 3 * gcols :] for piece in packed_pieces[:n_var]]
    else:
        second = exchange(second)
    g_qkv.append((full, pair_product(normed_send, full)))
    second_sum = add_all(*second)
    columns = [first_sum, second_sum]
    columns += [pair_own(normed_keep, full, swap_core(product)) for full, product in g_qkv]
    both_sum = jnp.concatenate(columns, axis=1)
    def my_slice(array, axis):
        return lax.dynamic_slice_in_dim(array, item * shard, shard, axis=axis)

    packed_pieces, both_sum = lax.optimization_barrier((packed_pieces, both_sum))
    both_rows = lax.psum_scatter(both_sum, "z", scatter_dimension=0, tiled=True)
    count = n_var
    if not lanes_fit:
        packed = [
            canonical(packed_pieces[part * n_var : (part + 1) * n_var]) for part in range(parts)
        ]
        packed = jnp.stack(packed, axis=0).reshape(parts, n_var, mine, 3, gcols)
        packed_pieces = [packed.transpose(2, 3, 1, 0, 4).reshape(mine, 3 * width)]
        count, parts = 1, 1
    packed_cols = 3 * gcols if lanes_fit else 3 * width

    far = pl.BlockSpec(memory_space=pl.ANY)
    table_rows = -(-(depth + 4) // 16) * 16
    late_rows = kept_rows + table_rows
    g_fields, late_send, late_keep = call(
        partial(back_kernel, count, parts, n_z),
        (1,),
        [pl.BlockSpec((block, packed_cols), lambda i, _: (i, 0)) for piece in packed_pieces]
        + [
            far,
            far,
            whole(gain_one.shape),
            far,
            far,
            pl.BlockSpec((depth, block), lambda i, _: (0, i)),
            whole(score_high.shape),
            whole(score_low.shape),
            whole((depth, HEADS * slots)),
            whole((depth, HEADS * slots)),
            whole(real.shape),
            whole(ev_back.shape),
            far,
            whole((2, width)),
        ],
        [
            pl.BlockSpec((depth, block), lambda i, _: (0, i)),
            whole((late_rows + HEADS, width)),
            whole((late_rows + HEADS, width)),
        ],
        [
            jax.ShapeDtypeStruct((depth, mine), bf16),
            jax.ShapeDtypeStruct((late_rows + HEADS, width), bf16),
            jax.ShapeDtypeStruct((late_rows + HEADS, width), f32),
        ],
        [
            pltpu.VMEM((HEADS * slots, block), bf16),
            pltpu.VMEM((block, 3 * width), bf16),
            pltpu.VMEM((table_rows, width), f32),
            pltpu.VMEM((depth, HEADS * slots), f32),
            pltpu.VMEM((3, width, width), bf16),
            pltpu.VMEM((mine, width), f32),
            pltpu.VMEM((mine, width), f32),
            pltpu.VMEM((width, width), bf16),
            pltpu.VMEM((width, mine), bf16),
            pltpu.SemaphoreType.DMA((7,)),
        ],
        cost(2 * mine * width * 4 * width, 8 * width * width + 20 * mine * width),
        "back",
        *packed_pieces, attn_qkv, merged, gain_one, g_stream, agg_out, pixels, score_high, score_low,
        score_high_t, score_low_t, real, ev_back, agg_values_t, gains_two,
    )

    late_send, mlp_out_rows = lax.optimization_barrier((late_send, mlp_out_rows))
    out_block = mlp_out_rows.shape[0] // n_var
    mlp_out_by = exchange(
        [
            lax.dynamic_slice_in_dim(mlp_out_rows, (me ^ d) * out_block, out_block, axis=0)
            for d in range(n_var)
        ]
    )
    mlp_out_rows = add_all(*mlp_out_by).reshape(shard, -1)

    late_got = swap_core(late_send)
    late_span = width // n_var
    n_blocks = -(-depth // late_span)
    n_spec = pl.BlockSpec((HEADS, n_blocks * late_span), lambda j, at: (late_rows // HEADS, 0))
    sum_rows = late_rows + n_blocks * HEADS
    f_rows = -(-channels * vars_here // 16) * 16
    piece_rows = sum_rows + f_rows * (mine // late_span)
    late_args = [late_keep, late_got]
    if late_span % 128:
        late_args = [
            jnp.take(array.reshape(-1, n_var, late_span).transpose(1, 0, 2), rel, axis=0)
            for array in late_args
        ]
    late_pieces = call(
        partial(pair_kernel, n_var, channels, vars_here, late_rows),
        (1,),
        [whole(array.shape) for array in late_args] + [n_spec, n_spec, whole((depth, mine))],
        [whole((piece_rows, late_span))] * n_var,
        [jax.ShapeDtypeStruct((piece_rows, late_span), bf16)] * n_var,
        [],
        cost(piece_rows * width, 8 * piece_rows * width),
        "late_pair",
        *late_args, late_keep, late_got, g_fields,
    )
    late_pieces = exchange(late_pieces)
    late_pieces, both_rows = lax.optimization_barrier((late_pieces, both_rows))
    rows_all = jnp.concatenate([both_rows, mlp_out_rows], axis=1)
    halves = 1 if n_var == 4 and lanes_fit else 0
    if halves:
        near = [send(rows_all, 1), send(rows_all, 2)]
    else:
        rows_all = list(lax.all_gather(rows_all, "var", axis=0))
    z_rows = shard + table_rows + n_blocks * HEADS
    *z_pieces, fields_grad = call(
        partial(z_pieces_kernel, n_var, shard, n_z),
        (1,),
        [whole((piece_rows, late_span))] * n_var,
        [whole((z_rows, late_span))] * n_z + [whole((f_rows, patches))],
        [jax.ShapeDtypeStruct((z_rows, late_span), bf16)] * n_z
        + [jax.ShapeDtypeStruct((f_rows, patches), f32)],
        [pltpu.VMEM((sum_rows, late_span), bf16)],
        cost(piece_rows * width, 2 * piece_rows * width),
        "late_z",
        *late_pieces,
    )
    z_pieces = [z_pieces[0]] + [send_z(z_pieces[d], d) for d in range(1, n_z)]
    late_rows_mine, n_all = pl.pallas_call(
        partial(z_sum_kernel, n_z),
        out_shape=[
            jax.ShapeDtypeStruct((shard + table_rows, late_span), bf16),
            jax.ShapeDtypeStruct((HEADS, n_blocks * late_span), f32),
        ],
        compiler_params=params(),
        cost_estimate=cost(z_rows * width, 2 * z_rows * width),
        name="late_sum",
    )(*z_pieces)

    fields_grad = fields_grad[: channels * vars_here].reshape(1, vars_here, channels, patches)
    if halves:
        late_rows_mine, near = lax.optimization_barrier((late_rows_mine, near))
        half = rows_all.shape[1] // 2
        rows_all = [rows_all] + near + [send(near[0][:, :half], 2), send(near[1][:, half:], 1)]
    late_by = exchange([late_rows_mine] * n_var)
    if late_span % 128:
        late_by = [canonical(late_by).transpose(1, 0, 2).reshape(shard + table_rows, width)]
    small_shapes = [(1, width), (channels * vars_here, shard), (vars_here, shard), (8, width)]
    final_in = [n_all, my_slice(tables, 1).T, spread, table_keys]
    item_rows = [
        pl.BlockSpec((shard, width), lambda i, at: (2 * at[2] + at[1], 0)),
        pl.BlockSpec((shard, HEADS), lambda i, at: (2 * at[2] + at[1], 0)),
    ]
    agg_out_grad, agg_value_grad, agg_key_grad, query_row, embed_weight_grad, var_embed_grad, gains = call(
        partial(final_kernel, len(late_by)),
        (1,),
        [whole(array.shape) for array in late_by + final_in] + item_rows,
        [whole((shard, width))] * 3
        + [whole(shape) for shape in small_shapes],
        [jax.ShapeDtypeStruct((shard, width), f32)] * 3
        + [jax.ShapeDtypeStruct(shape, f32) for shape in small_shapes],
        [pltpu.VMEM((table_rows, width), f32)],
        cost(2 * shard * width * 3 * depth, 12 * shard * width),
        "final",
        *late_by, *final_in, agg_value, query_keys,
    )
    gains = my_slice(gains, 1)
    agg_query_grad = my_slice(query_row[0], 0) * scale
    embed_weight_grad = embed_weight_grad.reshape(vars_here, channels, shard)

    row_shapes = [
        jax.ShapeDtypeStruct((shard, hidden_width), f32),
        jax.ShapeDtypeStruct((shard, width), f32),
        jax.ShapeDtypeStruct((shard, 3 * width), f32),
        jax.ShapeDtypeStruct((n_var, shard, out_block * width // shard), f32),
    ]
    mlp_in_grad, attn_proj_grad, attn_qkv_grad, mlp_out_grad = call(
        partial(assemble_kernel, n_var, here // group, gcols, halves),
        (1,),
        [whole(array.shape) for array in rows_all],
        [whole(row.shape) for row in row_shapes],
        row_shapes,
        [],
        cost(shard * 9 * width, 6 * shard * 9 * width),
        "assemble",
        *rows_all,
    )
    mlp_out_grad = mlp_out_grad.reshape(n_var * out_block, width)
    return (
        output[None],
        fields_grad,
        embed_weight_grad,
        var_embed_grad,
        agg_query_grad,
        agg_key_grad,
        agg_value_grad,
        agg_out_grad,
        gains[0],
        gains[1],
        attn_qkv_grad,
        attn_proj_grad,
        gains[2],
        gains[3],
        mlp_in_grad,
        mlp_out_grad,
    )


def solution(mesh):
    n_var, n_item = mesh.shape["var"], mesh.shape["item"]
    items = ("z", "core")
    return jax.shard_map(
        partial(per_device, n_var, n_item // 2),
        mesh=Mesh(mesh.devices.reshape(n_var, n_item // 2, 2), ("var", "z", "core")),
        in_specs=(
            P(items, "var", None, None),
            P(items, None),
            P("var", None, None),
            P("var", None),
            P(),
            P(),
            P(),
            P(),
            P(),
            P(),
            P(),
            P(),
            P(),
            P(),
            P(),
            P(),
            P(items, "var", None),
        ),
        out_specs=(
            P(items, "var", None),
            P(items, "var", None, None),
            P("var", None, items),
            P("var", items),
            P(items),
            P(items, None),
            P(items, None),
            P(items, None),
            P(items),
            P(items),
            P(items, None),
            P(items, None),
            P(items),
            P(items),
            P(items, None),
            P(items, None),
        ),
        check_vma=False,
    )
```

profile of v0, /device:TPU:0, one launch (start us, length us, event | category | flops | bytes accessed | tf_op | source)
XLA Modules:
  0.0 360.0 jit_solution(4146534363469000980)
XLA Ops:
  8.8 3.0 collective-permute-start
  19.5 7.1 %prep.1 = (bf16[80,2048]{1,0:T(8,128)(2,1)}, bf16[80,1024]{1,0:T(8,128)(2,1)}, bf16[256,80]{1,0:T(8,128)(2,1)}, bf16[256,80]{1,0:T(8,128)(2,1)}, bf16[80,256]{1,...) custom-call(s32[3]{0:T(128)} %pad_add_fusion.refs_0_.place_ref, ...), custom_call_target="tpu_custom_call" | custom-call | flops 33554432 | bytes 209715 | tf_op jit(solution)/shard_map/prep/pallas_call | solution.py:698
  26.6 23.5 %front.1 = (bf16[1024,512]{1,0:T(8,128)(2,1)}, f32[512,1024]{1,0:T(8,128)}, bf16[512,2048]{1,0:T(8,128)(2,1)}, bf16[512,2048]{1,0:T(8,128)(2,1)}, bf16[4,2048,64...) custom-call(s32[3]{0:T(128)} %pad_add_fusion.refs_0_.place_ref, ...), custom_call_target="tpu_custom_call" | custom-call | flops 429496736 | bytes 1677721 | tf_op jit(solution)/shard_map/front/pallas_call | solution.py:698
  50.1 8.6 %attend1.1 = (bf16[512,256]{1,0:T(8,128)(2,1)}, f32[4,1,512]{2,1,0:T(1,128)}) custom-call(bf16[4,2048,64]{2,1,0:T(8,128)(2,1)} %get-tuple-element.213.q_ref.refs_4_.refs_0_, bf16[4,2048,64]{2,1,0:T(8,128)(2,1)} %get-tuple-element.157.k_ref.refs_5_.refs_1_, bf16[4,2048,64]{2,1,0:T(8,128)(2,1)} %get-tuple-element.158.v_ref.refs_6_.refs_2_), custom_call_target="tpu_custom_call" | custom-call | flops 214748368 | bytes 209715 | tf_op jit(solution)/shard_map/attend1/pallas_call | solution.py:808
  58.7 8.6 %attend2.1 = (bf16[512,256]{1,0:T(8,128)(2,1)}, f32[4,1,512]{2,1,0:T(1,128)}) custom-call(bf16[4,2048,64]{2,1,0:T(8,128)(2,1)} %get-tuple-element.213.q_ref.refs_4_.refs_0_, bf16[4,2048,64]{2,1,0:T(8,128)(2,1)} %get-tuple-element.157.k_ref.refs_5_.refs_1_, bf16[4,2048,64]{2,1,0:T(8,128)(2,1)} %get-tuple-element.158.v_ref.refs_6_.refs_2_), custom_call_target="tpu_custom_call" | custom-call | flops 214748368 | bytes 209715 | tf_op jit(solution)/shard_map/attend2/pallas_call | solution.py:808
  67.3 8.9 %attend3.1 = (bf16[512,256]{1,0:T(8,128)(2,1)}, f32[4,1,512]{2,1,0:T(1,128)}) custom-call(bf16[4,2048,64]{2,1,0:T(8,128)(2,1)} %get-tuple-element.213.q_ref.refs_4_.refs_0_, bf16[4,2048,64]{2,1,0:T(8,128)(2,1)} %get-tuple-element.157.k_ref.refs_5_.refs_1_, bf16[4,2048,64]{2,1,0:T(8,128)(2,1)} %get-tuple-element.158.v_ref.refs_6_.refs_2_), custom_call_target="tpu_custom_call" | custom-call | flops 214748368 | bytes 209715 | tf_op jit(solution)/shard_map/attend3/pallas_call | solution.py:808
  79.7 8.6 %attend0.1 = (bf16[512,256]{1,0:T(8,128)(2,1)}, f32[4,1,512]{2,1,0:T(1,128)}) custom-call(bf16[4,2048,64]{2,1,0:T(8,128)(2,1)} %get-tuple-element.213.q_ref.refs_4_.refs_0_, bf16[4,2048,64]{2,1,0:T(8,128)(2,1)} %get-tuple-element.157.k_ref.refs_5_.refs_1_, bf16[4,2048,64]{2,1,0:T(8,128)(2,1)} %get-tuple-element.158.v_ref.refs_6_.refs_2_), custom_call_target="tpu_custom_call" | custom-call | flops 214748368 | bytes 209715 | tf_op jit(solution)/shard_map/attend0/pallas_call | solution.py:808
  90.3 32.2 %mlp.1 = (bf16[512,1024]{1,0:T(8,128)(2,1)}, bf16[1024,512]{1,0:T(8,128)(2,1)}, bf16[1024,512]{1,0:T(8,128)(2,1)}, bf16[2048,512]{1,0:T(8,128)(2,1)}, bf16[2048,...) custom-call(s32[3]{0:T(128)} %pad_add_fusion.refs_0_.place_ref, ...), custom_call_target="tpu_custom_call" | custom-call | flops 966367616 | bytes 1258291 | tf_op jit(solution)/shard_map/mlp/pallas_call | solution.py:698
  126.0 8.6 %send.1 = bf16[512,5120]{1,0:T(8,128)(2,1)} custom-call(s32[3]{0:T(128)} %pad_add_fusion.refs_0_.place_ref, bf16[4,2,128,512]{3,2,1,0:T(8,128)(2,1)} %bitcast.57, bf16[512,4096]{1,0:T(8,128)(2,1)} %get-tuple-element.167.main_cols.refs_2_, bf16[4,2,128,512]{3,2,1,0:T(8,128)(2,1)} %bitcast.55, bf16[512,1024]{1,0:T(8,128)(2,1)} %get-tuple-element.169.side_cols.refs_5_), custom_call_target="tpu_custom_call" | custom-call | flops 5368709120 | bytes 25165824 | tf_op jit(solution)/shard_map/send/pallas_call | solution.py:698
  134.9 4.3 %convolution_convert_fusion = bf16[2048,1024]{1,0:T(8,128)(2,1)} fusion(bf16[2048,512]{1,0:T(8,128)(2,1)S(1)} %copy-done.35, bf16[1,512,1024]{2,1,0:T(8,128)(2,1)S(1)} %copy-done.8), kind=kOutput, calls=%fused_computation.1 | convolution fusion | flops 2149580800 | bytes 7340032 | tf_op jit(solution)/shard_map/dot_general | solution.py:25
  139.8 4.1 %collective-permute-done.9.refs_3_.refs_6_ = bf16[512,5120]{1,0:T(8,128)(2,1)} collective-permute-done((bf16[512,5120]{1,0:T(8,128)(2,1)}, bf16[512,5120]{1,0:T(8,128)(2,1)}, u32[]{:S(2)}, u32[]{:S(2)}) %collective-permute-start.9) | collective-permute-done | bytes 5242912 | tf_op jit(solution)/shard_map/ppermute | solution.py:692
  143.9 10.1 %keep.1 = (bf16[512,768]{1,0:T(8,128)(2,1)}, bf16[512,768]{1,0:T(8,128)(2,1)}, bf16[512,768]{1,0:T(8,128)(2,1)}, bf16[512,768]{1,0:T(8,128)(2,1)}, bf16[512,512]...) custom-call(s32[3]{0:T(128)} %pad_add_fusion.refs_0_.place_ref, ...), custom_call_target="tpu_custom_call" | custom-call | flops 5368709120 | bytes 25165824 | tf_op jit(solution)/shard_map/keep/pallas_call | solution.py:698
  154.0 3.9 %fusion.7 = f32[2048,1024]{1,0:T(8,128)S(1)} fusion(bf16[2048,512]{1,0:T(8,128)(2,1)} %get-tuple-element.196, bf16[1,512,1024]{2,1,0:T(8,128)(2,1)S(1)} %copy-done.8), kind=kOutput, calls=%fused_computation.31 | convolution fusion | flops 2147483648 | bytes 11534336 | tf_op jit(solution)/shard_map/dot_general | solution.py:25
  157.9 3.6 %add_convert_fusion = bf16[2048,1024]{1,0:T(8,128)(2,1)} fusion(f32[2048,1024]{1,0:T(8,128)S(1)} %fusion.7, bf16[2048,1024]{1,0:T(8,128)(2,1)S(1)} %collective-permute-done.10), kind=kLoop, calls=%fused_computation | loop fusion | flops 6291456 | bytes 16777216 | tf_op jit(solution)/shard_map/convert_element_type | solution.py:914
  165.3 28.4 %attend_back0.1 = (bf16[2048,384]{1,0:T(8,128)(2,1)}, bf16[512,896]{1,0:T(8,128)(2,1)}, bf16[512,896]{1,0:T(8,128)(2,1)}, bf16[512,896]{1,0:T(8,128)(2,1)}, bf16[512,896]{1,0:T(8,128)(2,1)}) custom-call(bf16[512,512]{1,0:T(8,128)(2,1)} %get-tuple-element.184.refs_0_, bf16[512,512]{1,0:T(8,128)(2,1)} %get-tuple-element.185.refs_1_, ...), custom_call_target="tpu_custom_call" | custom-call | flops 1073741824 | bytes 209715 | tf_op jit(solution)/shard_map/attend_back0/pallas_call | solution.py:1005
  202.4 26.9 %attend_back1.1 = (bf16[2048,384]{1,0:T(8,128)(2,1)}, bf16[512,384]{1,0:T(8,128)(2,1)}, bf16[512,384]{1,0:T(8,128)(2,1)}, bf16[512,384]{1,0:T(8,128)(2,1)}, bf16[512,384]{1,0:T(8,128)(2,1)}) custom-call(bf16[4,2048,64]{2,1,0:T(8,128)(2,1)} %get-tuple-element.213.q_ref.refs_4_.refs_0_, bf16[4,2048,64]{2,1,0:T(8,128)(2,1)} %get-tuple-element.157.k_ref.refs_5_.refs_1_, ...), custom_call_target="tpu_custom_call" | custom-call | flops 1073741824 | bytes 209715 | tf_op jit(solution)/shard_map/attend_back1/pallas_call | solution.py:1005
  229.3 2.8 convolution_convert_fusion.1
  232.7 4.7 %collective-permute-done.15.refs_3_ = bf16[512,896]{1,0:T(8,128)(2,1)S(1)} collective-permute-done((bf16[512,896]{1,0:T(8,128)(2,1)}, bf16[512,896]{1,0:T(8,128)(2,1)S(1)}, u32[]{:S(2)}, u32[]{:S(2)}) %collective-permute-start.15) | collective-permute-done | bytes 917536 | tf_op jit(solution)/shard_map/ppermute | solution.py:686
  246.5 4.2 %collective-permute-done.17.refs_6_ = bf16[512,384]{1,0:T(8,128)(2,1)S(1)} collective-permute-done((bf16[512,384]{1,0:T(8,128)(2,1)}, bf16[512,384]{1,0:T(8,128)(2,1)S(1)}, u32[]{:S(2)}, u32[]{:S(2)}) %collective-permute-start.17) | collective-permute-done | bytes 393248 | tf_op jit(solution)/shard_map/ppermute | solution.py:686
  250.7 8.3 %collective-permute-done.18.refs_7_ = bf16[512,384]{1,0:T(8,128)(2,1)S(1)} collective-permute-done((bf16[512,384]{1,0:T(8,128)(2,1)}, bf16[512,384]{1,0:T(8,128)(2,1)S(1)}, u32[]{:S(2)}, u32[]{:S(2)}) %collective-permute-start.18) | collective-permute-done | bytes 393248 | tf_op jit(solution)/shard_map/ppermute | solution.py:686
  259.7 17.4 %back.1 = (bf16[80,512]{1,0:T(8,128)(2,1)}, bf16[624,1024]{1,0:T(8,128)(2,1)}, f32[624,1024]{1,0:T(8,128)}) custom-call(s32[3]{0:T(128)} %pad_add_fusion.refs_0_.place_ref, bf16[512,896]{1,0:T(8,128)(2,1)} %get-tuple-element.234.refs_1_, bf16[512,896]{1,0:T(8,128)(2,1)} %copy-done.3, bf16[512,896]{1,0:T(8,128)(2,1)} %copy-done.4, ...), custom_call_target="tpu_custom_call" | custom-call | flops 214748368 | bytes 943718 | tf_op jit(solution)/shard_map/back/pallas_call | solution.py:698
  279.9 2.2 collective-permute-start.29
  283.1 4.1 %late_pair.1 = (bf16[656,256]{1,0:T(8,128)(2,1)}, bf16[656,256]{1,0:T(8,128)(2,1)}, bf16[656,256]{1,0:T(8,128)(2,1)}, bf16[656,256]{1,0:T(8,128)(2,1)}) custom-call(s32[3]{0:T(128)} %pad_add_fusion.refs_0_.place_ref, f32[624,1024]{1,0:T(8,128)} %get-tuple-element.248.refs_1_.refs_3_, bf16[624,1024]{1,0:T(8,128)(2,1)} %copy-done, ...), custom_call_target="tpu_custom_call" | custom-call | flops 33587 | bytes 268697 | tf_op jit(solution)/shard_map/late_pair/pallas_call | solution.py:698
  290.7 3.1 collective-permute-done.30
  295.1 8.1 %reduce-scatter.5.cloned.1.call-done = bf16[128,2048]{1,0:T(8,128)(2,1)} async-done(((bf16[512,2048]{1,0:T(8,128)(2,1)}), bf16[128,2048]{1,0:T(8,128)(2,1)}) %reduce-scatter.5.cloned.1.call-update) | async-done | bytes 524304 | tf_op jit(solution)/shard_map/reduce_scatter | solution.py:1062
  303.2 5.0 %collective-permute-done.25.refs_4_ = bf16[656,256]{1,0:T(8,128)(2,1)S(1)} collective-permute-done((bf16[656,256]{1,0:T(8,128)(2,1)}, bf16[656,256]{1,0:T(8,128)(2,1)S(1)}, u32[]{:S(2)}, u32[]{:S(2)}) %collective-permute-start.25) | collective-permute-done | bytes 335904 | tf_op jit(solution)/shard_map/ppermute | solution.py:686
  311.1 3.1 late_z.1
  315.6 2.6 collective-permute-start.27
  318.5 2.1 collective-permute-done.26.refs_1_
  320.6 6.8 %collective-permute-done.27.refs_2_ = bf16[240,256]{1,0:T(8,128)(2,1)S(1)} collective-permute-done((bf16[240,256]{1,0:T(8,128)(2,1)}, bf16[240,256]{1,0:T(8,128)(2,1)S(1)}, u32[]{:S(2)}, u32[]{:S(2)}) %collective-permute-start.27) | collective-permute-done | bytes 122912 | tf_op jit(solution)/shard_map/ppermute | solution.py:689
  339.8 3.6 final.1
  347.3 5.6 %assemble.1 = (f32[128,4096]{1,0:T(8,128)}, f32[128,1024]{1,0:T(8,128)}, f32[128,3072]{1,0:T(8,128)}, f32[4,128,1024]{2,1,0:T(8,128)}) custom-call(s32[3]{0:T(128)} %pad_add_fusion.refs_0_.place_ref, bf16[128,3072]{1,0:T(8,128)(2,1)} %copy-done.1, bf16[128,3072]{1,0:T(8,128)(2,1)} %copy-done.6, bf16[128,3072]{1,0:T(8,128)(2,1)} %copy-done.7, ...), custom_call_target="tpu_custom_call" | custom-call | flops 58982 | bytes 353894 | tf_op jit(solution)/shard_map/assemble/pallas_call | solution.py:698
  (179 shorter events, 71.2 us)
Async XLA Ops:
  7.2 270.0 %reduce-scatter.3.cloned.1.call-start = ((), (), s32[]{:S(2)}) async-start(), calls=%async_computation.2 | async-start | bytes 5242880 | tf_op jit(solution)/shard_map/reduce_scatter | solution.py:993
  76.2 12.1 %collective-permute-start.3 = (bf16[512,256]{1,0:T(8,128)(2,1)S(1)}, bf16[512,256]{1,0:T(8,128)(2,1)S(1)}, u32[]{:S(2)}, u32[]{:S(2)}) collective-permute-start(bf16[512,256]{1,0:T(8,128)(2,1)S(1)} %copy-done.9), channel_id=1, source_target_pairs={{0,8},{8,0},{16,24},{24,16},{1,9},{9,1},{17,25},{25,17},{2,10},{10... | collective-permute-start | bytes 786440 | tf_op jit(solution)/shard_map/ppermute | solution.py:686
  76.8 12.7 %collective-permute-start.4 = (bf16[512,256]{1,0:T(8,128)(2,1)S(1)}, bf16[512,256]{1,0:T(8,128)(2,1)S(1)}, u32[]{:S(2)}, u32[]{:S(2)}) collective-permute-start(bf16[512,256]{1,0:T(8,128)(2,1)S(1)} %copy-done.10), channel_id=1, source_target_pairs={{0,16},{8,24},{16,0},{24,8},{1,17},{9,25},{17,1},{25,9},{2,18},{10... | collective-permute-start | bytes 786440 | tf_op jit(solution)/shard_map/ppermute | solution.py:686
  78.3 11.2 %collective-permute-start.5 = (bf16[512,256]{1,0:T(8,128)(2,1)}, bf16[512,256]{1,0:T(8,128)(2,1)S(1)}, u32[]{:S(2)}, u32[]{:S(2)}) collective-permute-start(bf16[512,256]{1,0:T(8,128)(2,1)} %get-tuple-element.162.refs_14_.refs_10_), channel_id=1, source_target_pairs={{0,24},{8,16},{16,8},{24,0},{1,25},{9,17},{17,9},{25,1},{2,26},{10... | collective-permute-start | bytes 786440 | tf_op jit(solution)/shard_map/ppermute | solution.py:686
  122.5 12.2 %collective-permute-start.6 = (bf16[512,256]{1,0:T(8,128)(2,1)}, bf16[512,256]{1,0:T(8,128)(2,1)S(1)}, u32[]{:S(2)}, u32[]{:S(2)}) collective-permute-start(bf16[512,256]{1,0:T(8,128)(2,1)} %get-tuple-element.171), channel_id=1, source_target_pairs={{0,8},{8,0},{16,24},{24,16},{1,9},{9,1},{17,25},{25,17},{2,10},{10... | collective-permute-start | bytes 786440 | tf_op jit(solution)/shard_map/ppermute | solution.py:686
  123.3 11.6 %collective-permute-start.7 = (bf16[512,256]{1,0:T(8,128)(2,1)}, bf16[512,256]{1,0:T(8,128)(2,1)S(1)}, u32[]{:S(2)}, u32[]{:S(2)}) collective-permute-start(bf16[512,256]{1,0:T(8,128)(2,1)} %get-tuple-element.172), channel_id=1, source_target_pairs={{0,16},{8,24},{16,0},{24,8},{1,17},{9,25},{17,1},{25,9},{2,18},{10... | collective-permute-start | bytes 786440 | tf_op jit(solution)/shard_map/ppermute | solution.py:686
  124.8 10.0 %collective-permute-start.8 = (bf16[512,256]{1,0:T(8,128)(2,1)}, bf16[512,256]{1,0:T(8,128)(2,1)S(1)}, u32[]{:S(2)}, u32[]{:S(2)}) collective-permute-start(bf16[512,256]{1,0:T(8,128)(2,1)} %get-tuple-element.173), channel_id=1, source_target_pairs={{0,24},{8,16},{16,8},{24,0},{1,25},{9,17},{17,9},{25,1},{2,26},{10... | collective-permute-start | bytes 786440 | tf_op jit(solution)/shard_map/ppermute | solution.py:686
  139.2 18.7 %collective-permute-start.10 = (bf16[2048,1024]{1,0:T(8,128)(2,1)}, bf16[2048,1024]{1,0:T(8,128)(2,1)S(1)}, u32[]{:S(2)}, u32[]{:S(2)}) collective-permute-start(bf16[2048,1024]{1,0:T(8,128)(2,1)} %convolution_convert_fusion), channel_id=1, source_target_pairs={{0,1},{1,0},{2,3},{3,2},{4,5},{5,4},{6,7},{7,6},{8,9},{9,8},{10,11... | collective-permute-start | bytes 12582920 | tf_op jit(solution)/shard_map/ppermute | solution.py:692
  161.6 141.6 %reduce-scatter.5.cloned.1.call-start = ((), (), s32[]{:S(2)}) async-start(), calls=%async_computation.3 | async-start | bytes 2621440 | tf_op jit(solution)/shard_map/reduce_scatter | solution.py:1062
  161.6 34.2 %collective-permute-start.11 = (bf16[512,768]{1,0:T(8,128)(2,1)}, bf16[512,768]{1,0:T(8,128)(2,1)S(1)}, u32[]{:S(2)}, u32[]{:S(2)}) collective-permute-start(bf16[512,768]{1,0:T(8,128)(2,1)} %get-tuple-element.204), channel_id=1, source_target_pairs={{0,8},{8,0},{16,24},{24,16},{1,9},{9,1},{17,25},{25,17},{2,10},{10... | collective-permute-start | bytes 2359304 | tf_op jit(solution)/shard_map/ppermute | solution.py:686
  162.9 35.3 %collective-permute-start.12 = (bf16[512,768]{1,0:T(8,128)(2,1)S(1)}, bf16[512,768]{1,0:T(8,128)(2,1)S(1)}, u32[]{:S(2)}, u32[]{:S(2)}) collective-permute-start(bf16[512,768]{1,0:T(8,128)(2,1)S(1)} %copy-done.40), channel_id=1, source_target_pairs={{0,16},{8,24},{16,0},{24,8},{1,17},{9,25},{17,1},{25,9},{2,18},{10... | collective-permute-start | bytes 2359304 | tf_op jit(solution)/shard_map/ppermute | solution.py:686
  164.0 35.9 %collective-permute-start.13 = (bf16[512,768]{1,0:T(8,128)(2,1)S(1)}, bf16[512,768]{1,0:T(8,128)(2,1)S(1)}, u32[]{:S(2)}, u32[]{:S(2)}) collective-permute-start(bf16[512,768]{1,0:T(8,128)(2,1)S(1)} %copy-done.39), channel_id=1, source_target_pairs={{0,24},{8,16},{16,8},{24,0},{1,25},{9,17},{17,9},{25,1},{2,26},{10... | collective-permute-start | bytes 2359304 | tf_op jit(solution)/shard_map/ppermute | solution.py:686
  193.7 39.0 %collective-permute-start.14 = (bf16[512,896]{1,0:T(8,128)(2,1)}, bf16[512,896]{1,0:T(8,128)(2,1)S(1)}, u32[]{:S(2)}, u32[]{:S(2)}) collective-permute-start(bf16[512,896]{1,0:T(8,128)(2,1)} %get-tuple-element.219), channel_id=1, source_target_pairs={{0,8},{8,0},{16,24},{24,16},{1,9},{9,1},{17,25},{25,17},{2,10},{10... | collective-permute-start | bytes 2752520 | tf_op jit(solution)/shard_map/ppermute | solution.py:686
  194.7 42.7 %collective-permute-start.15 = (bf16[512,896]{1,0:T(8,128)(2,1)}, bf16[512,896]{1,0:T(8,128)(2,1)S(1)}, u32[]{:S(2)}, u32[]{:S(2)}) collective-permute-start(bf16[512,896]{1,0:T(8,128)(2,1)} %get-tuple-element.220), channel_id=1, source_target_pairs={{0,16},{8,24},{16,0},{24,8},{1,17},{9,25},{17,1},{25,9},{2,18},{10... | collective-permute-start | bytes 2752520 | tf_op jit(solution)/shard_map/ppermute | solution.py:686
  195.8 42.6 %collective-permute-start.16 = (bf16[512,896]{1,0:T(8,128)(2,1)}, bf16[512,896]{1,0:T(8,128)(2,1)S(1)}, u32[]{:S(2)}, u32[]{:S(2)}) collective-permute-start(bf16[512,896]{1,0:T(8,128)(2,1)} %get-tuple-element.221), channel_id=1, source_target_pairs={{0,24},{8,16},{16,8},{24,0},{1,25},{9,17},{17,9},{25,1},{2,26},{10... | collective-permute-start | bytes 2752520 | tf_op jit(solution)/shard_map/ppermute | solution.py:686
  232.1 10.1 %collective-permute-start.21 = (bf16[512,384]{1,0:T(8,128)(2,1)S(1)}, bf16[512,384]{1,0:T(8,128)(2,1)S(1)}, u32[]{:S(2)}, u32[]{:S(2)}) collective-permute-start(bf16[512,384]{1,0:T(8,128)(2,1)S(1)} %convolution_convert_fusion.1), channel_id=1, source_target_pairs={{0,1},{1,0},{2,3},{3,2},{4,5},{5,4},{6,7},{7,6},{8,9},{9,8},{10,11... | collective-permute-start | bytes 1179656 | tf_op jit(solution)/shard_map/ppermute | solution.py:692
  232.2 11.4 %collective-permute-start.20 = (bf16[512,384]{1,0:T(8,128)(2,1)}, bf16[512,384]{1,0:T(8,128)(2,1)S(1)}, u32[]{:S(2)}, u32[]{:S(2)}) collective-permute-start(bf16[512,384]{1,0:T(8,128)(2,1)} %convolution_convert_fusion.2), channel_id=1, source_target_pairs={{0,1},{1,0},{2,3},{3,2},{4,5},{5,4},{6,7},{7,6},{8,9},{9,8},{10,11... | collective-permute-start | bytes 1179656 | tf_op jit(solution)/shard_map/ppermute | solution.py:692
  238.5 12.3 %collective-permute-start.17 = (bf16[512,384]{1,0:T(8,128)(2,1)}, bf16[512,384]{1,0:T(8,128)(2,1)S(1)}, u32[]{:S(2)}, u32[]{:S(2)}) collective-permute-start(bf16[512,384]{1,0:T(8,128)(2,1)} %get-tuple-element.227), channel_id=1, source_target_pairs={{0,8},{8,0},{16,24},{24,16},{1,9},{9,1},{17,25},{25,17},{2,10},{10... | collective-permute-start | bytes 1179656 | tf_op jit(solution)/shard_map/ppermute | solution.py:686
  239.7 19.3 %collective-permute-start.18 = (bf16[512,384]{1,0:T(8,128)(2,1)}, bf16[512,384]{1,0:T(8,128)(2,1)S(1)}, u32[]{:S(2)}, u32[]{:S(2)}) collective-permute-start(bf16[512,384]{1,0:T(8,128)(2,1)} %get-tuple-element.228), channel_id=1, source_target_pairs={{0,16},{8,24},{16,0},{24,8},{1,17},{9,25},{17,1},{25,9},{2,18},{10... | collective-permute-start | bytes 1179656 | tf_op jit(solution)/shard_map/ppermute | solution.py:686
  240.7 18.3 %collective-permute-start.19 = (bf16[512,384]{1,0:T(8,128)(2,1)}, bf16[512,384]{1,0:T(8,128)(2,1)}, u32[]{:S(2)}, u32[]{:S(2)}) collective-permute-start(bf16[512,384]{1,0:T(8,128)(2,1)} %get-tuple-element.229), channel_id=1, source_target_pairs={{0,24},{8,16},{16,8},{24,0},{1,25},{9,17},{17,9},{25,1},{2,26},{10... | collective-permute-start | bytes 1179656 | tf_op jit(solution)/shard_map/ppermute | solution.py:686
  278.5 10.3 %collective-permute-start.31 = (bf16[128,1024]{1,0:T(8,128)(2,1)S(1)}, bf16[128,1024]{1,0:T(8,128)(2,1)S(1)}, u32[]{:S(2)}, u32[]{:S(2)}) collective-permute-start(bf16[128,1024]{1,0:T(8,128)(2,1)S(1)} %get-tuple-element.289), channel_id=1, source_target_pairs={{0,24},{8,16},{16,8},{24,0},{1,25},{9,17},{17,9},{25,1},{2,26},{10... | collective-permute-start | bytes 786440 | tf_op jit(solution)/shard_map/ppermute | solution.py:686
  279.6 14.3 %collective-permute-start.30 = (bf16[128,1024]{1,0:T(8,128)(2,1)S(1)}, bf16[128,1024]{1,0:T(8,128)(2,1)S(1)}, u32[]{:S(2)}, u32[]{:S(2)}) collective-permute-start(bf16[128,1024]{1,0:T(8,128)(2,1)S(1)} %get-tuple-element.290), channel_id=1, source_target_pairs={{0,16},{8,24},{16,0},{24,8},{1,17},{9,25},{17,1},{25,9},{2,18},{10... | collective-permute-start | bytes 786440 | tf_op jit(solution)/shard_map/ppermute | solution.py:686
  279.9 13.9 %collective-permute-start.29 = (bf16[128,1024]{1,0:T(8,128)(2,1)S(1)}, bf16[128,1024]{1,0:T(8,128)(2,1)}, u32[]{:S(2)}, u32[]{:S(2)}) collective-permute-start(bf16[128,1024]{1,0:T(8,128)(2,1)S(1)} %get-tuple-element.288), channel_id=1, source_target_pairs={{0,8},{8,0},{16,24},{24,16},{1,9},{9,1},{17,25},{25,17},{2,10},{10... | collective-permute-start | bytes 786440 | tf_op jit(solution)/shard_map/ppermute | solution.py:686
  287.2 15.9 %collective-permute-start.23 = (bf16[656,256]{1,0:T(8,128)(2,1)}, bf16[656,256]{1,0:T(8,128)(2,1)S(1)}, u32[]{:S(2)}, u32[]{:S(2)}) collective-permute-start(bf16[656,256]{1,0:T(8,128)(2,1)} %get-tuple-element.253), channel_id=1, source_target_pairs={{0,8},{8,0},{16,24},{24,16},{1,9},{9,1},{17,25},{25,17},{2,10},{10... | collective-permute-start | bytes 1007624 | tf_op jit(solution)/shard_map/ppermute | solution.py:686
  287.3 15.9 %collective-permute-start.24 = (bf16[656,256]{1,0:T(8,128)(2,1)}, bf16[656,256]{1,0:T(8,128)(2,1)S(1)}, u32[]{:S(2)}, u32[]{:S(2)}) collective-permute-start(bf16[656,256]{1,0:T(8,128)(2,1)} %get-tuple-element.254), channel_id=1, source_target_pairs={{0,16},{8,24},{16,0},{24,8},{1,17},{9,25},{17,1},{25,9},{2,18},{10... | collective-permute-start | bytes 1007624 | tf_op jit(solution)/shard_map/ppermute | solution.py:686
  288.8 19.4 %collective-permute-start.25 = (bf16[656,256]{1,0:T(8,128)(2,1)}, bf16[656,256]{1,0:T(8,128)(2,1)S(1)}, u32[]{:S(2)}, u32[]{:S(2)}) collective-permute-start(bf16[656,256]{1,0:T(8,128)(2,1)} %get-tuple-element.255), channel_id=1, source_target_pairs={{0,24},{8,16},{16,8},{24,0},{1,25},{9,17},{17,9},{25,1},{2,26},{10... | collective-permute-start | bytes 1007624 | tf_op jit(solution)/shard_map/ppermute | solution.py:686
  309.4 20.5 %collective-permute-start.32 = (bf16[128,3072]{1,0:T(8,128)(2,1)S(1)}, bf16[128,3072]{1,0:T(8,128)(2,1)S(1)}, u32[]{:S(2)}, u32[]{:S(2)}) collective-permute-start(bf16[128,3072]{1,0:T(8,128)(2,1)S(1)} %pad_maximum_fusion.1.refs_1_), channel_id=1, source_target_pairs={{0,8},{8,0},{16,24},{24,16},{1,9},{9,1},{17,25},{25,17},{2,10},{10... | collective-permute-start | bytes 2359304 | tf_op jit(solution)/shard_map/ppermute | solution.py:686
  309.5 20.4 %collective-permute-start.33 = (bf16[128,3072]{1,0:T(8,128)(2,1)S(1)}, bf16[128,3072]{1,0:T(8,128)(2,1)S(1)}, u32[]{:S(2)}, u32[]{:S(2)}) collective-permute-start(bf16[128,3072]{1,0:T(8,128)(2,1)S(1)} %pad_maximum_fusion.1.refs_1_), channel_id=1, source_target_pairs={{0,16},{8,24},{16,0},{24,8},{1,17},{9,25},{17,1},{25,9},{2,18},{10... | collective-permute-start | bytes 2359304 | tf_op jit(solution)/shard_map/ppermute | solution.py:686
  315.6 11.8 %collective-permute-start.27 = (bf16[240,256]{1,0:T(8,128)(2,1)}, bf16[240,256]{1,0:T(8,128)(2,1)S(1)}, u32[]{:S(2)}, u32[]{:S(2)}) collective-permute-start(bf16[240,256]{1,0:T(8,128)(2,1)} %get-tuple-element.264), channel_id=1, source_target_pairs={{0,4},{2,6},{4,0},{6,2},{1,5},{3,7},{5,1},{7,3},{8,12},{10,14},{12... | collective-permute-start | bytes 368648 | tf_op jit(solution)/shard_map/ppermute | solution.py:689
  330.0 9.8 %collective-permute-start.34 = (bf16[224,256]{1,0:T(8,128)(2,1)}, bf16[224,256]{1,0:T(8,128)(2,1)}, u32[]{:S(2)}, u32[]{:S(2)}) collective-permute-start(bf16[224,256]{1,0:T(8,128)(2,1)} %get-tuple-element.269.refs_1_), channel_id=1, source_target_pairs={{0,8},{8,0},{16,24},{24,16},{1,9},{9,1},{17,25},{25,17},{2,10},{10... | collective-permute-start | bytes 344072 | tf_op jit(solution)/shard_map/ppermute | solution.py:686
  334.4 12.2 %collective-permute-start.37 = (bf16[128,1536]{1,0:T(8,128)(2,1)S(1)}, bf16[128,1536]{1,0:T(8,128)(2,1)S(1)}, u32[]{:S(2)}, u32[]{:S(2)}) collective-permute-start(bf16[128,1536]{1,0:T(8,128)(2,1)S(1)} %slice.40), channel_id=1, source_target_pairs={{0,16},{8,24},{16,0},{24,8},{1,17},{9,25},{17,1},{25,9},{2,18},{10... | collective-permute-start | bytes 1179656 | tf_op jit(solution)/shard_map/ppermute | solution.py:686
  335.1 11.5 %collective-permute-start.38 = (bf16[128,1536]{1,0:T(8,128)(2,1)S(1)}, bf16[128,1536]{1,0:T(8,128)(2,1)}, u32[]{:S(2)}, u32[]{:S(2)}) collective-permute-start(bf16[128,1536]{1,0:T(8,128)(2,1)S(1)} %slice.41), channel_id=1, source_target_pairs={{0,8},{8,0},{16,24},{24,16},{1,9},{9,1},{17,25},{25,17},{2,10},{10... | collective-permute-start | bytes 1179656 | tf_op jit(solution)/shard_map/ppermute | solution.py:686
  (50 other events, 410.4 us)
Sparse Core Ops, SparseCore 0:
  161.7 77.0 reduce-scatter.2
  259.1 43.9 reduce-scatter.4
where the time goes:
time: 366 us; the launch traced here: 360 us
  Pallas kernels  207 us (57%)
  waiting for transfers between devices  53.9 us (15%)
  starting transfers between devices  42.7 us (12%)
  matrix products  15.6 us (4%)
  between operations  14.7 us (4%)
  local copies, waits for them, and re-layouts  14.5 us (4%)
  other arithmetic  11.6 us (3%)
    pallas_call x10, Pallas kernels, call(): pl.pallas_call(kernel, grid_spec=pltpu.PrefetchScalarGridSpec(num_scalar_...  115 us
    pallas_call x2, Pallas kernels, attend_back(): pl.pallas_call(partial(attend_back_kernel, n_var, len(extra)), grid=(patc...  55.3 us
    ppermute x31, starting transfers between devices, send(): return lax.ppermute(array, 'var', [(i, i ^ other) for i in range(n_var)])  37 us
    pallas_call x4, Pallas kernels, attend(): pl.pallas_call(attend_kernel, grid=(here // heads,), in_specs=[pl.BlockSp...  34.7 us
    ppermute x31, waiting for transfers between devices, send(): return lax.ppermute(array, 'var', [(i, i ^ other) for i in range(n_var)])  32.7 us
    dot_general x6, matrix products, dot(): lax.dot_general(a, b, (((1,), (0,)), ((), ())), preferred_element_type=f32)  15.6 us
    ppermute x3, waiting for transfers between devices, send_z(): return lax.ppermute(array, 'z', [(i, i ^ other) for i in range(n_z)])  8.93 us
    reduce_scatter x1, waiting for transfers between devices, per_device(): both_rows = lax.psum_scatter(both_sum, 'z', scatter_dimension=0, tiled=True)  8.09 us
  transfers between devices with their start and end apart: 41, of which 16 were waited for; matrix products, arithmetic and copies ran while one was open for 8% of the time, Pallas kernels for 29%

commit v1 on v0

--- a/solution.py
+++ b/solution.py
@@ -451,8 +451,9 @@
     pieces, outs, fields_ref, total_s = refs[1 : 1 + count], refs[1 + count : -2], refs[-2], refs[-1]
     me, z_at = refs[0][0], refs[0][2]
     rows, span = total_s.shape
-    f_rows = fields_ref.shape[0]
-    mine = fields_ref.shape[1] // count
+    vars_here, channels, patches = fields_ref.shape
+    mine = patches // count
+    f_rows = (pieces[0].shape[0] - rows) // (mine // span)
     total = pieces[0][:rows].astype(f32)
     for piece in pieces[1:]:
         total = total + piece[:rows].astype(f32)
@@ -466,7 +467,9 @@
             pieces[d][rows + b * f_rows : rows + (b + 1) * f_rows] for b in range(mine // span)
         ]
         at = pl.multiple_of((me ^ d) * mine, mine)
-        fields_ref[:, pl.ds(at, mine)] = jnp.concatenate(blocks, axis=1).astype(f32)
+        block = jnp.concatenate(blocks, axis=1).astype(f32)
+        for v in range(vars_here):
+            fields_ref[v, :, pl.ds(at, mine)] = block[v * channels : (v + 1) * channels]
 
 
 def assemble_kernel(count, parts, size, halves, *refs):
@@ -513,7 +516,8 @@
     place_ref = refs[0]
     pieces = refs[1 : 1 + count]
     n_ref, tables_ref, spread_ref, keys_ref, value_ref, qk_ref = refs[1 + count : 7 + count]
-    outg_ref, valg_ref, keyg_ref, queryg_ref, embedg_ref, varg_ref, gains_ref, m_s = refs[7 + count :]
+    outg_ref, valg_ref, keyg_ref, embedg_ref, varg_ref = refs[7 + count : 12 + count]
+    *row_refs, m_s, row_s = refs[12 + count :]
     shard, depth = tables_ref.shape
     width = m_s.shape[1]
     for d in range(count):
@@ -533,7 +537,7 @@
     same = head_at == lax.broadcasted_iota(jnp.int32, (HEADS, width), 0)
     ones = jnp.where(same, 1.0, 0.0).astype(bf16)
     n_wide = dot(n_high.astype(f32).T.astype(bf16), ones) + dot(n_low.astype(f32).T.astype(bf16), ones)
-    queryg_ref[...] = jnp.sum(n_wide * keys_ref[...], axis=0, keepdims=True)
+    row_s[4:5] = jnp.sum(n_wide * keys_ref[...], axis=0, keepdims=True) * (width // HEADS) ** (-0.5)
     qk = qk_ref[...]
     table_grad = split_three(
         dot_nt(m_low, value_ref[...])
@@ -542,13 +546,24 @@
     )
     slots = depth // TABLES
     vars_here = varg_ref.shape[0]
-    for ref, first, each in ((embedg_ref, 0, TABLES - 1), (varg_ref, TABLES - 1, 1)):
+    for first, each in ((0, TABLES - 1), (TABLES - 1, 1)):
         row = lax.broadcasted_iota(jnp.int32, (each * vars_here, depth), 0)
         col = lax.broadcasted_iota(jnp.int32, (each * vars_here, depth), 1)
         want = (first + row % each) * slots + place_ref[0] * vars_here + row // each
         picks = jnp.where(want == col, 1.0, 0.0).astype(bf16)
-        ref[...] = sum(dot(picks, part) for part in table_grad)
-    gains_ref[...] = m_s[depth : depth + 8, :]
+        rows = sum(dot(picks, part) for part in table_grad)
+        if each == 1:
+            varg_ref[...] = rows
+        else:
+            for v in range(vars_here):
+                embedg_ref[v] = rows[v * each : (v + 1) * each]
+    row_s[0:4] = m_s[depth : depth + 4, :]
+    at = (2 * place_ref[2] + place_ref[1]) * shard
+    for i, ref in enumerate(row_refs):
+        if shard % 128:
+            ref[...] = row_s[i : i + 1]
+        else:
+            ref[...] = row_s[i : i + 1, pl.ds(pl.multiple_of(at, shard), shard)]
 
 
 def back_kernel(count, parts, n_z, *refs):
@@ -1168,9 +1183,9 @@
         partial(z_pieces_kernel, n_var, shard, n_z),
         (1,),
         [whole((piece_rows, late_span))] * n_var,
-        [whole((z_rows, late_span))] * n_z + [whole((f_rows, patches))],
+        [whole((z_rows, late_span))] * n_z + [whole((vars_here, channels, patches))],
         [jax.ShapeDtypeStruct((z_rows, late_span), bf16)] * n_z
-        + [jax.ShapeDtypeStruct((f_rows, patches), f32)],
+        + [jax.ShapeDtypeStruct((vars_here, channels, patches), f32)],
         [pltpu.VMEM((sum_rows, late_span), bf16)],
         cost(piece_rows * width, 2 * piece_rows * width),
         "late_z",
@@ -1188,7 +1203,7 @@
         name="late_sum",
     )(*z_pieces)
 
-    fields_grad = fields_grad[: channels * vars_here].reshape(1, vars_here, channels, patches)
+    fields_grad = fields_grad[None]
     if halves:
         late_rows_mine, near = lax.optimization_barrier((late_rows_mine, near))
         half = rows_all.shape[1] // 2
@@ -1196,13 +1211,14 @@
     late_by = exchange([late_rows_mine] * n_var)
     if late_span % 128:
         late_by = [canonical(late_by).transpose(1, 0, 2).reshape(shard + table_rows, width)]
-    small_shapes = [(1, width), (channels * vars_here, shard), (vars_here, shard), (8, width)]
+    row_width = width if shard % 128 else shard
+    small_shapes = [(vars_here, channels, shard), (vars_here, shard)] + [(1, row_width)] * 5
     final_in = [n_all, my_slice(tables, 1).T, spread, table_keys]
     item_rows = [
         pl.BlockSpec((shard, width), lambda i, at: (2 * at[2] + at[1], 0)),
         pl.BlockSpec((shard, HEADS), lambda i, at: (2 * at[2] + at[1], 0)),
     ]
-    agg_out_grad, agg_value_grad, agg_key_grad, query_row, embed_weight_grad, var_embed_grad, gains = call(
+    agg_out_grad, agg_value_grad, agg_key_grad, embed_weight_grad, var_embed_grad, *rows = call(
         partial(final_kernel, len(late_by)),
         (1,),
         [whole(array.shape) for array in late_by + final_in] + item_rows,
@@ -1210,14 +1226,14 @@
         + [whole(shape) for shape in small_shapes],
         [jax.ShapeDtypeStruct((shard, width), f32)] * 3
         + [jax.ShapeDtypeStruct(shape, f32) for shape in small_shapes],
-        [pltpu.VMEM((table_rows, width), f32)],
+        [pltpu.VMEM((table_rows, width), f32), pltpu.VMEM((8, width), f32)],
         cost(2 * shard * width * 3 * depth, 12 * shard * width),
         "final",
         *late_by, *final_in, agg_value, query_keys,
     )
-    gains = my_slice(gains, 1)
-    agg_query_grad = my_slice(query_row[0], 0) * scale
-    embed_weight_grad = embed_weight_grad.reshape(vars_here, channels, shard)
+    *gains, agg_query_grad = [
+        row[0] if row_width == shard else my_slice(row[0], 0) for row in rows
+    ]
 
     row_shapes = [
         jax.ShapeDtypeStruct((shard, hidden_width), f32),

time: 366 us -> 368 us (level)
  waiting for transfers between devices: 53.9 us -> 59.5 us
    ppermute x31, waiting for transfers between devices: 32.7 us -> 38.3 us  [send(): return lax.ppermute(array, 'var', [(i, i ^ other) for i in range(n_var)])]
  transfers between devices with their start and end apart: 41 -> 41, of which waited for: 16 -> 18; matrix products, arithmetic and copies ran while one was open for 8% -> 7% of each run, Pallas kernels for 29% -> 29%
where the time goes in v1:
time: 368 us; the launch traced here: 362 us
  Pallas kernels  207 us (56%)
  waiting for transfers between devices  59.5 us (16%)
  starting transfers between devices  42.9 us (12%)
  matrix products  15.5 us (4%)
  between operations  14.8 us (4%)
  local copies, waits for them, and re-layouts  11.9 us (3%)
  other arithmetic  10.4 us (3%)
    pallas_call x10, Pallas kernels, call(): pl.pallas_call(kernel, grid_spec=pltpu.PrefetchScalarGridSpec(num_scalar_...  115 us
    pallas_call x2, Pallas kernels, attend_back(): pl.pallas_call(partial(attend_back_kernel, n_var, len(extra)), grid=(patc...  55.3 us
    ppermute x31, waiting for transfers between devices, send(): return lax.ppermute(array, 'var', [(i, i ^ other) for i in range(n_var)])  38.3 us
    ppermute x31, starting transfers between devices, send(): return lax.ppermute(array, 'var', [(i, i ^ other) for i in range(n_var)])  37.2 us
    pallas_call x4, Pallas kernels, attend(): pl.pallas_call(attend_kernel, grid=(here // heads,), in_specs=[pl.BlockSp...  34.7 us
    dot_general x6, matrix products, dot(): lax.dot_general(a, b, (((1,), (0,)), ((), ())), preferred_element_type=f32)  15.5 us
    ppermute x3, waiting for transfers between devices, send_z(): return lax.ppermute(array, 'z', [(i, i ^ other) for i in range(n_z)])  8.84 us
    reduce_scatter x1, waiting for transfers between devices, per_device(): both_rows = lax.psum_scatter(both_sum, 'z', scatter_dimension=0, tiled=True)  8.14 us
  transfers between devices with their start and end apart: 41, of which 18 were waited for; matrix products, arithmetic and copies ran while one was open for 7% of the time, Pallas kernels for 29%

profile of v1, /device:TPU:0, one launch (start us, length us, event | category | flops | bytes accessed | tf_op | source)
XLA Modules:
  0.0 361.8 jit_solution(16723074959394294014)
XLA Ops:
  8.8 3.0 collective-permute-start
  19.5 7.1 %prep.1 = (bf16[80,2048]{1,0:T(8,128)(2,1)}, bf16[80,1024]{1,0:T(8,128)(2,1)}, bf16[256,80]{1,0:T(8,128)(2,1)}, bf16[256,80]{1,0:T(8,128)(2,1)}, bf16[80,256]{1,...) custom-call(s32[3]{0:T(128)} %pad_add_fusion.refs_0_.place_ref, ...), custom_call_target="tpu_custom_call" | custom-call | flops 33554432 | bytes 209715 | tf_op jit(solution)/shard_map/prep/pallas_call | solution.py:713
  26.6 23.5 %front.1 = (bf16[1024,512]{1,0:T(8,128)(2,1)}, f32[512,1024]{1,0:T(8,128)}, bf16[512,2048]{1,0:T(8,128)(2,1)}, bf16[512,2048]{1,0:T(8,128)(2,1)}, bf16[4,2048,64...) custom-call(s32[3]{0:T(128)} %pad_add_fusion.refs_0_.place_ref, ...), custom_call_target="tpu_custom_call" | custom-call | flops 429496736 | bytes 1677721 | tf_op jit(solution)/shard_map/front/pallas_call | solution.py:713
  50.1 8.6 %attend1.1 = (bf16[512,256]{1,0:T(8,128)(2,1)}, f32[4,1,512]{2,1,0:T(1,128)}) custom-call(bf16[4,2048,64]{2,1,0:T(8,128)(2,1)} %get-tuple-element.216.q_ref.refs_4_.refs_0_, bf16[4,2048,64]{2,1,0:T(8,128)(2,1)} %get-tuple-element.160.k_ref.refs_5_.refs_1_, bf16[4,2048,64]{2,1,0:T(8,128)(2,1)} %get-tuple-element.161.v_ref.refs_6_.refs_2_), custom_call_target="tpu_custom_call" | custom-call | flops 214748368 | bytes 209715 | tf_op jit(solution)/shard_map/attend1/pallas_call | solution.py:823
  58.7 8.6 %attend2.1 = (bf16[512,256]{1,0:T(8,128)(2,1)}, f32[4,1,512]{2,1,0:T(1,128)}) custom-call(bf16[4,2048,64]{2,1,0:T(8,128)(2,1)} %get-tuple-element.216.q_ref.refs_4_.refs_0_, bf16[4,2048,64]{2,1,0:T(8,128)(2,1)} %get-tuple-element.160.k_ref.refs_5_.refs_1_, bf16[4,2048,64]{2,1,0:T(8,128)(2,1)} %get-tuple-element.161.v_ref.refs_6_.refs_2_), custom_call_target="tpu_custom_call" | custom-call | flops 214748368 | bytes 209715 | tf_op jit(solution)/shard_map/attend2/pallas_call | solution.py:823
  67.3 8.9 %attend3.1 = (bf16[512,256]{1,0:T(8,128)(2,1)}, f32[4,1,512]{2,1,0:T(1,128)}) custom-call(bf16[4,2048,64]{2,1,0:T(8,128)(2,1)} %get-tuple-element.216.q_ref.refs_4_.refs_0_, bf16[4,2048,64]{2,1,0:T(8,128)(2,1)} %get-tuple-element.160.k_ref.refs_5_.refs_1_, bf16[4,2048,64]{2,1,0:T(8,128)(2,1)} %get-tuple-element.161.v_ref.refs_6_.refs_2_), custom_call_target="tpu_custom_call" | custom-call | flops 214748368 | bytes 209715 | tf_op jit(solution)/shard_map/attend3/pallas_call | solution.py:823
  79.7 8.6 %attend0.1 = (bf16[512,256]{1,0:T(8,128)(2,1)}, f32[4,1,512]{2,1,0:T(1,128)}) custom-call(bf16[4,2048,64]{2,1,0:T(8,128)(2,1)} %get-tuple-element.216.q_ref.refs_4_.refs_0_, bf16[4,2048,64]{2,1,0:T(8,128)(2,1)} %get-tuple-element.160.k_ref.refs_5_.refs_1_, bf16[4,2048,64]{2,1,0:T(8,128)(2,1)} %get-tuple-element.161.v_ref.refs_6_.refs_2_), custom_call_target="tpu_custom_call" | custom-call | flops 214748368 | bytes 209715 | tf_op jit(solution)/shard_map/attend0/pallas_call | solution.py:823
  90.3 32.2 %mlp.1 = (bf16[512,1024]{1,0:T(8,128)(2,1)}, bf16[1024,512]{1,0:T(8,128)(2,1)}, bf16[1024,512]{1,0:T(8,128)(2,1)}, bf16[2048,512]{1,0:T(8,128)(2,1)}, bf16[2048,...) custom-call(s32[3]{0:T(128)} %pad_add_fusion.refs_0_.place_ref, ...), custom_call_target="tpu_custom_call" | custom-call | flops 966367616 | bytes 1258291 | tf_op jit(solution)/shard_map/mlp/pallas_call | solution.py:713
  126.0 8.6 %send.1 = bf16[512,5120]{1,0:T(8,128)(2,1)} custom-call(s32[3]{0:T(128)} %pad_add_fusion.refs_0_.place_ref, bf16[4,2,128,512]{3,2,1,0:T(8,128)(2,1)} %bitcast.51, bf16[512,4096]{1,0:T(8,128)(2,1)} %get-tuple-element.170.main_cols.refs_2_, bf16[4,2,128,512]{3,2,1,0:T(8,128)(2,1)} %bitcast.49, bf16[512,1024]{1,0:T(8,128)(2,1)} %get-tuple-element.172.side_cols.refs_5_), custom_call_target="tpu_custom_call" | custom-call | flops 5368709120 | bytes 25165824 | tf_op jit(solution)/shard_map/send/pallas_call | solution.py:713
  134.9 4.3 %convolution_convert_fusion = bf16[2048,1024]{1,0:T(8,128)(2,1)} fusion(bf16[2048,512]{1,0:T(8,128)(2,1)S(1)} %copy-done.34, bf16[1,512,1024]{2,1,0:T(8,128)(2,1)S(1)} %copy-done.8), kind=kOutput, calls=%fused_computation.1 | convolution fusion | flops 2149580800 | bytes 7340032 | tf_op jit(solution)/shard_map/dot_general | solution.py:25
  139.8 4.1 %collective-permute-done.9.refs_3_.refs_6_ = bf16[512,5120]{1,0:T(8,128)(2,1)} collective-permute-done((bf16[512,5120]{1,0:T(8,128)(2,1)}, bf16[512,5120]{1,0:T(8,128)(2,1)}, u32[]{:S(2)}, u32[]{:S(2)}) %collective-permute-start.9) | collective-permute-done | bytes 5242912 | tf_op jit(solution)/shard_map/ppermute | solution.py:707
  143.9 10.1 %keep.1 = (bf16[512,768]{1,0:T(8,128)(2,1)}, bf16[512,768]{1,0:T(8,128)(2,1)}, bf16[512,768]{1,0:T(8,128)(2,1)}, bf16[512,768]{1,0:T(8,128)(2,1)}, bf16[512,512]...) custom-call(s32[3]{0:T(128)} %pad_add_fusion.refs_0_.place_ref, ...), custom_call_target="tpu_custom_call" | custom-call | flops 5368709120 | bytes 25165824 | tf_op jit(solution)/shard_map/keep/pallas_call | solution.py:713
  154.0 3.9 %fusion.5 = f32[2048,1024]{1,0:T(8,128)S(1)} fusion(bf16[2048,512]{1,0:T(8,128)(2,1)} %get-tuple-element.199, bf16[1,512,1024]{2,1,0:T(8,128)(2,1)S(1)} %copy-done.8), kind=kOutput, calls=%fused_computation.23 | convolution fusion | flops 2147483648 | bytes 11534336 | tf_op jit(solution)/shard_map/dot_general | solution.py:25
  157.9 3.6 add_convert_fusion
  165.3 28.4 %attend_back0.1 = (bf16[2048,384]{1,0:T(8,128)(2,1)}, bf16[512,896]{1,0:T(8,128)(2,1)}, bf16[512,896]{1,0:T(8,128)(2,1)}, bf16[512,896]{1,0:T(8,128)(2,1)}, bf16[512,896]{1,0:T(8,128)(2,1)}) custom-call(bf16[512,512]{1,0:T(8,128)(2,1)} %get-tuple-element.187.refs_0_, bf16[512,512]{1,0:T(8,128)(2,1)} %get-tuple-element.188.refs_1_, ...), custom_call_target="tpu_custom_call" | custom-call | flops 1073741824 | bytes 209715 | tf_op jit(solution)/shard_map/attend_back0/pallas_call | solution.py:1020
  202.3 26.9 %attend_back1.1 = (bf16[2048,384]{1,0:T(8,128)(2,1)}, bf16[512,384]{1,0:T(8,128)(2,1)}, bf16[512,384]{1,0:T(8,128)(2,1)}, bf16[512,384]{1,0:T(8,128)(2,1)}, bf16[512,384]{1,0:T(8,128)(2,1)}) custom-call(bf16[4,2048,64]{2,1,0:T(8,128)(2,1)} %get-tuple-element.216.q_ref.refs_4_.refs_0_, bf16[4,2048,64]{2,1,0:T(8,128)(2,1)} %get-tuple-element.160.k_ref.refs_5_.refs_1_, ...), custom_call_target="tpu_custom_call" | custom-call | flops 1073741824 | bytes 209715 | tf_op jit(solution)/shard_map/attend_back1/pallas_call | solution.py:1020
  229.3 2.8 convolution_convert_fusion.1
  232.7 4.8 %collective-permute-done.15.refs_3_ = bf16[512,896]{1,0:T(8,128)(2,1)S(1)} collective-permute-done((bf16[512,896]{1,0:T(8,128)(2,1)}, bf16[512,896]{1,0:T(8,128)(2,1)S(1)}, u32[]{:S(2)}, u32[]{:S(2)}) %collective-permute-start.15) | collective-permute-done | bytes 917536 | tf_op jit(solution)/shard_map/ppermute | solution.py:701
  246.5 4.2 %collective-permute-done.17.refs_6_ = bf16[512,384]{1,0:T(8,128)(2,1)S(1)} collective-permute-done((bf16[512,384]{1,0:T(8,128)(2,1)}, bf16[512,384]{1,0:T(8,128)(2,1)S(1)}, u32[]{:S(2)}, u32[]{:S(2)}) %collective-permute-start.17) | collective-permute-done | bytes 393248 | tf_op jit(solution)/shard_map/ppermute | solution.py:701
  250.7 8.2 %collective-permute-done.18.refs_7_ = bf16[512,384]{1,0:T(8,128)(2,1)S(1)} collective-permute-done((bf16[512,384]{1,0:T(8,128)(2,1)}, bf16[512,384]{1,0:T(8,128)(2,1)S(1)}, u32[]{:S(2)}, u32[]{:S(2)}) %collective-permute-start.18) | collective-permute-done | bytes 393248 | tf_op jit(solution)/shard_map/ppermute | solution.py:701
  259.7 17.4 %back.1 = (bf16[80,512]{1,0:T(8,128)(2,1)}, bf16[624,1024]{1,0:T(8,128)(2,1)}, f32[624,1024]{1,0:T(8,128)}) custom-call(s32[3]{0:T(128)} %pad_add_fusion.refs_0_.place_ref, bf16[512,896]{1,0:T(8,128)(2,1)} %get-tuple-element.237.refs_1_, bf16[512,896]{1,0:T(8,128)(2,1)} %copy-done.3, bf16[512,896]{1,0:T(8,128)(2,1)} %copy-done.4, ...), custom_call_target="tpu_custom_call" | custom-call | flops 214748368 | bytes 943718 | tf_op jit(solution)/shard_map/back/pallas_call | solution.py:713
  279.9 2.1 collective-permute-start.29
  283.1 4.1 %late_pair.1 = (bf16[656,256]{1,0:T(8,128)(2,1)}, bf16[656,256]{1,0:T(8,128)(2,1)}, bf16[656,256]{1,0:T(8,128)(2,1)}, bf16[656,256]{1,0:T(8,128)(2,1)}) custom-call(s32[3]{0:T(128)} %pad_add_fusion.refs_0_.place_ref, f32[624,1024]{1,0:T(8,128)} %get-tuple-element.251.refs_1_.refs_3_, bf16[624,1024]{1,0:T(8,128)(2,1)} %copy-done, ...), custom_call_target="tpu_custom_call" | custom-call | flops 33587 | bytes 268697 | tf_op jit(solution)/shard_map/late_pair/pallas_call | solution.py:713
  290.7 3.1 collective-permute-done.30
  295.0 8.1 %reduce-scatter.5.cloned.1.call-done = bf16[128,2048]{1,0:T(8,128)(2,1)} async-done(((bf16[512,2048]{1,0:T(8,128)(2,1)}), bf16[128,2048]{1,0:T(8,128)(2,1)}) %reduce-scatter.5.cloned.1.call-update) | async-done | bytes 524304 | tf_op jit(solution)/shard_map/reduce_scatter | solution.py:1077
  303.2 5.0 %collective-permute-done.25.refs_4_ = bf16[656,256]{1,0:T(8,128)(2,1)S(1)} collective-permute-done((bf16[656,256]{1,0:T(8,128)(2,1)}, bf16[656,256]{1,0:T(8,128)(2,1)S(1)}, u32[]{:S(2)}, u32[]{:S(2)}) %collective-permute-start.25) | collective-permute-done | bytes 335904 | tf_op jit(solution)/shard_map/ppermute | solution.py:701
  311.0 3.0 late_z.1
  315.0 2.6 collective-permute-start.27
  320.5 6.8 %collective-permute-done.27.refs_2_ = bf16[240,256]{1,0:T(8,128)(2,1)S(1)} collective-permute-done((bf16[240,256]{1,0:T(8,128)(2,1)}, bf16[240,256]{1,0:T(8,128)(2,1)S(1)}, u32[]{:S(2)}, u32[]{:S(2)}) %collective-permute-start.27) | collective-permute-done | bytes 122912 | tf_op jit(solution)/shard_map/ppermute | solution.py:704
  339.1 4.0 %collective-permute-done.34.refs_2_ = bf16[224,256]{1,0:T(8,128)(2,1)} collective-permute-done((bf16[224,256]{1,0:T(8,128)(2,1)}, bf16[224,256]{1,0:T(8,128)(2,1)}, u32[]{:S(2)}, u32[]{:S(2)}) %collective-permute-start.34) | collective-permute-done | bytes 114720 | tf_op jit(solution)/shard_map/ppermute | solution.py:701
  344.8 3.6 final.1
  349.2 5.6 %assemble.1 = (f32[128,4096]{1,0:T(8,128)}, f32[128,1024]{1,0:T(8,128)}, f32[128,3072]{1,0:T(8,128)}, f32[4,128,1024]{2,1,0:T(8,128)}) custom-call(s32[3]{0:T(128)} %pad_add_fusion.refs_0_.place_ref, bf16[128,3072]{1,0:T(8,128)(2,1)} %copy-done.1, bf16[128,3072]{1,0:T(8,128)(2,1)} %copy-done.6, bf16[128,3072]{1,0:T(8,128)(2,1)} %copy-done.7, ...), custom_call_target="tpu_custom_call" | custom-call | flops 58982 | bytes 353894 | tf_op jit(solution)/shard_map/assemble/pallas_call | solution.py:713
  (173 shorter events, 71.2 us)
Async XLA Ops:
  7.2 270.0 %reduce-scatter.3.cloned.1.call-start = ((), (), s32[]{:S(2)}) async-start(), calls=%async_computation.2 | async-start | bytes 5242880 | tf_op jit(solution)/shard_map/reduce_scatter | solution.py:1008
  76.2 12.1 %collective-permute-start.3 = (bf16[512,256]{1,0:T(8,128)(2,1)S(1)}, bf16[512,256]{1,0:T(8,128)(2,1)S(1)}, u32[]{:S(2)}, u32[]{:S(2)}) collective-permute-start(bf16[512,256]{1,0:T(8,128)(2,1)S(1)} %copy-done.9), channel_id=1, source_target_pairs={{0,8},{8,0},{16,24},{24,16},{1,9},{9,1},{17,25},{25,17},{2,10},{10... | collective-permute-start | bytes 786440 | tf_op jit(solution)/shard_map/ppermute | solution.py:701
  76.8 12.7 %collective-permute-start.4 = (bf16[512,256]{1,0:T(8,128)(2,1)S(1)}, bf16[512,256]{1,0:T(8,128)(2,1)S(1)}, u32[]{:S(2)}, u32[]{:S(2)}) collective-permute-start(bf16[512,256]{1,0:T(8,128)(2,1)S(1)} %copy-done.10), channel_id=1, source_target_pairs={{0,16},{8,24},{16,0},{24,8},{1,17},{9,25},{17,1},{25,9},{2,18},{10... | collective-permute-start | bytes 786440 | tf_op jit(solution)/shard_map/ppermute | solution.py:701
  78.3 11.2 %collective-permute-start.5 = (bf16[512,256]{1,0:T(8,128)(2,1)}, bf16[512,256]{1,0:T(8,128)(2,1)S(1)}, u32[]{:S(2)}, u32[]{:S(2)}) collective-permute-start(bf16[512,256]{1,0:T(8,128)(2,1)} %get-tuple-element.165.refs_14_.refs_10_), channel_id=1, source_target_pairs={{0,24},{8,16},{16,8},{24,0},{1,25},{9,17},{17,9},{25,1},{2,26},{10... | collective-permute-start | bytes 786440 | tf_op jit(solution)/shard_map/ppermute | solution.py:701
  122.5 12.2 %collective-permute-start.6 = (bf16[512,256]{1,0:T(8,128)(2,1)}, bf16[512,256]{1,0:T(8,128)(2,1)S(1)}, u32[]{:S(2)}, u32[]{:S(2)}) collective-permute-start(bf16[512,256]{1,0:T(8,128)(2,1)} %get-tuple-element.174), channel_id=1, source_target_pairs={{0,8},{8,0},{16,24},{24,16},{1,9},{9,1},{17,25},{25,17},{2,10},{10... | collective-permute-start | bytes 786440 | tf_op jit(solution)/shard_map/ppermute | solution.py:701
  123.3 11.5 %collective-permute-start.7 = (bf16[512,256]{1,0:T(8,128)(2,1)}, bf16[512,256]{1,0:T(8,128)(2,1)S(1)}, u32[]{:S(2)}, u32[]{:S(2)}) collective-permute-start(bf16[512,256]{1,0:T(8,128)(2,1)} %get-tuple-element.175), channel_id=1, source_target_pairs={{0,16},{8,24},{16,0},{24,8},{1,17},{9,25},{17,1},{25,9},{2,18},{10... | collective-permute-start | bytes 786440 | tf_op jit(solution)/shard_map/ppermute | solution.py:701
  139.2 18.7 %collective-permute-start.10 = (bf16[2048,1024]{1,0:T(8,128)(2,1)}, bf16[2048,1024]{1,0:T(8,128)(2,1)S(1)}, u32[]{:S(2)}, u32[]{:S(2)}) collective-permute-start(bf16[2048,1024]{1,0:T(8,128)(2,1)} %convolution_convert_fusion), channel_id=1, source_target_pairs={{0,1},{1,0},{2,3},{3,2},{4,5},{5,4},{6,7},{7,6},{8,9},{9,8},{10,11... | collective-permute-start | bytes 12582920 | tf_op jit(solution)/shard_map/ppermute | solution.py:707
  161.5 141.6 %reduce-scatter.5.cloned.1.call-start = ((), (), s32[]{:S(2)}) async-start(), calls=%async_computation.3 | async-start | bytes 2621440 | tf_op jit(solution)/shard_map/reduce_scatter | solution.py:1077
  161.6 34.3 %collective-permute-start.11 = (bf16[512,768]{1,0:T(8,128)(2,1)}, bf16[512,768]{1,0:T(8,128)(2,1)S(1)}, u32[]{:S(2)}, u32[]{:S(2)}) collective-permute-start(bf16[512,768]{1,0:T(8,128)(2,1)} %get-tuple-element.207), channel_id=1, source_target_pairs={{0,8},{8,0},{16,24},{24,16},{1,9},{9,1},{17,25},{25,17},{2,10},{10... | collective-permute-start | bytes 2359304 | tf_op jit(solution)/shard_map/ppermute | solution.py:701
  162.9 35.4 %collective-permute-start.12 = (bf16[512,768]{1,0:T(8,128)(2,1)S(1)}, bf16[512,768]{1,0:T(8,128)(2,1)S(1)}, u32[]{:S(2)}, u32[]{:S(2)}) collective-permute-start(bf16[512,768]{1,0:T(8,128)(2,1)S(1)} %copy-done.39), channel_id=1, source_target_pairs={{0,16},{8,24},{16,0},{24,8},{1,17},{9,25},{17,1},{25,9},{2,18},{10... | collective-permute-start | bytes 2359304 | tf_op jit(solution)/shard_map/ppermute | solution.py:701
  164.0 35.9 %collective-permute-start.13 = (bf16[512,768]{1,0:T(8,128)(2,1)S(1)}, bf16[512,768]{1,0:T(8,128)(2,1)S(1)}, u32[]{:S(2)}, u32[]{:S(2)}) collective-permute-start(bf16[512,768]{1,0:T(8,128)(2,1)S(1)} %copy-done.38), channel_id=1, source_target_pairs={{0,24},{8,16},{16,8},{24,0},{1,25},{9,17},{17,9},{25,1},{2,26},{10... | collective-permute-start | bytes 2359304 | tf_op jit(solution)/shard_map/ppermute | solution.py:701
  193.7 38.9 %collective-permute-start.14 = (bf16[512,896]{1,0:T(8,128)(2,1)}, bf16[512,896]{1,0:T(8,128)(2,1)S(1)}, u32[]{:S(2)}, u32[]{:S(2)}) collective-permute-start(bf16[512,896]{1,0:T(8,128)(2,1)} %get-tuple-element.222), channel_id=1, source_target_pairs={{0,8},{8,0},{16,24},{24,16},{1,9},{9,1},{17,25},{25,17},{2,10},{10... | collective-permute-start | bytes 2752520 | tf_op jit(solution)/shard_map/ppermute | solution.py:701
  194.7 42.7 %collective-permute-start.15 = (bf16[512,896]{1,0:T(8,128)(2,1)}, bf16[512,896]{1,0:T(8,128)(2,1)S(1)}, u32[]{:S(2)}, u32[]{:S(2)}) collective-permute-start(bf16[512,896]{1,0:T(8,128)(2,1)} %get-tuple-element.223), channel_id=1, source_target_pairs={{0,16},{8,24},{16,0},{24,8},{1,17},{9,25},{17,1},{25,9},{2,18},{10... | collective-permute-start | bytes 2752520 | tf_op jit(solution)/shard_map/ppermute | solution.py:701
  195.8 42.6 %collective-permute-start.16 = (bf16[512,896]{1,0:T(8,128)(2,1)}, bf16[512,896]{1,0:T(8,128)(2,1)S(1)}, u32[]{:S(2)}, u32[]{:S(2)}) collective-permute-start(bf16[512,896]{1,0:T(8,128)(2,1)} %get-tuple-element.224), channel_id=1, source_target_pairs={{0,24},{8,16},{16,8},{24,0},{1,25},{9,17},{17,9},{25,1},{2,26},{10... | collective-permute-start | bytes 2752520 | tf_op jit(solution)/shard_map/ppermute | solution.py:701
  232.2 11.4 %collective-permute-start.20 = (bf16[512,384]{1,0:T(8,128)(2,1)}, bf16[512,384]{1,0:T(8,128)(2,1)S(1)}, u32[]{:S(2)}, u32[]{:S(2)}) collective-permute-start(bf16[512,384]{1,0:T(8,128)(2,1)} %convolution_convert_fusion.2), channel_id=1, source_target_pairs={{0,1},{1,0},{2,3},{3,2},{4,5},{5,4},{6,7},{7,6},{8,9},{9,8},{10,11... | collective-permute-start | bytes 1179656 | tf_op jit(solution)/shard_map/ppermute | solution.py:707
  238.4 12.3 %collective-permute-start.17 = (bf16[512,384]{1,0:T(8,128)(2,1)}, bf16[512,384]{1,0:T(8,128)(2,1)S(1)}, u32[]{:S(2)}, u32[]{:S(2)}) collective-permute-start(bf16[512,384]{1,0:T(8,128)(2,1)} %get-tuple-element.230), channel_id=1, source_target_pairs={{0,8},{8,0},{16,24},{24,16},{1,9},{9,1},{17,25},{25,17},{2,10},{10... | collective-permute-start | bytes 1179656 | tf_op jit(solution)/shard_map/ppermute | solution.py:701
  239.7 19.3 %collective-permute-start.18 = (bf16[512,384]{1,0:T(8,128)(2,1)}, bf16[512,384]{1,0:T(8,128)(2,1)S(1)}, u32[]{:S(2)}, u32[]{:S(2)}) collective-permute-start(bf16[512,384]{1,0:T(8,128)(2,1)} %get-tuple-element.231), channel_id=1, source_target_pairs={{0,16},{8,24},{16,0},{24,8},{1,17},{9,25},{17,1},{25,9},{2,18},{10... | collective-permute-start | bytes 1179656 | tf_op jit(solution)/shard_map/ppermute | solution.py:701
  240.6 18.3 %collective-permute-start.19 = (bf16[512,384]{1,0:T(8,128)(2,1)}, bf16[512,384]{1,0:T(8,128)(2,1)}, u32[]{:S(2)}, u32[]{:S(2)}) collective-permute-start(bf16[512,384]{1,0:T(8,128)(2,1)} %get-tuple-element.232), channel_id=1, source_target_pairs={{0,24},{8,16},{16,8},{24,0},{1,25},{9,17},{17,9},{25,1},{2,26},{10... | collective-permute-start | bytes 1179656 | tf_op jit(solution)/shard_map/ppermute | solution.py:701
  278.4 10.3 %collective-permute-start.31 = (bf16[128,1024]{1,0:T(8,128)(2,1)S(1)}, bf16[128,1024]{1,0:T(8,128)(2,1)S(1)}, u32[]{:S(2)}, u32[]{:S(2)}) collective-permute-start(bf16[128,1024]{1,0:T(8,128)(2,1)S(1)} %get-tuple-element.295), channel_id=1, source_target_pairs={{0,24},{8,16},{16,8},{24,0},{1,25},{9,17},{17,9},{25,1},{2,26},{10... | collective-permute-start | bytes 786440 | tf_op jit(solution)/shard_map/ppermute | solution.py:701
  279.5 14.3 %collective-permute-start.30 = (bf16[128,1024]{1,0:T(8,128)(2,1)S(1)}, bf16[128,1024]{1,0:T(8,128)(2,1)S(1)}, u32[]{:S(2)}, u32[]{:S(2)}) collective-permute-start(bf16[128,1024]{1,0:T(8,128)(2,1)S(1)} %get-tuple-element.296), channel_id=1, source_target_pairs={{0,16},{8,24},{16,0},{24,8},{1,17},{9,25},{17,1},{25,9},{2,18},{10... | collective-permute-start | bytes 786440 | tf_op jit(solution)/shard_map/ppermute | solution.py:701
  279.9 13.9 %collective-permute-start.29 = (bf16[128,1024]{1,0:T(8,128)(2,1)S(1)}, bf16[128,1024]{1,0:T(8,128)(2,1)}, u32[]{:S(2)}, u32[]{:S(2)}) collective-permute-start(bf16[128,1024]{1,0:T(8,128)(2,1)S(1)} %get-tuple-element.294), channel_id=1, source_target_pairs={{0,8},{8,0},{16,24},{24,16},{1,9},{9,1},{17,25},{25,17},{2,10},{10... | collective-permute-start | bytes 786440 | tf_op jit(solution)/shard_map/ppermute | solution.py:701
  287.2 16.0 %collective-permute-start.23 = (bf16[656,256]{1,0:T(8,128)(2,1)}, bf16[656,256]{1,0:T(8,128)(2,1)S(1)}, u32[]{:S(2)}, u32[]{:S(2)}) collective-permute-start(bf16[656,256]{1,0:T(8,128)(2,1)} %get-tuple-element.256), channel_id=1, source_target_pairs={{0,8},{8,0},{16,24},{24,16},{1,9},{9,1},{17,25},{25,17},{2,10},{10... | collective-permute-start | bytes 1007624 | tf_op jit(solution)/shard_map/ppermute | solution.py:701
  287.2 15.9 %collective-permute-start.24 = (bf16[656,256]{1,0:T(8,128)(2,1)}, bf16[656,256]{1,0:T(8,128)(2,1)S(1)}, u32[]{:S(2)}, u32[]{:S(2)}) collective-permute-start(bf16[656,256]{1,0:T(8,128)(2,1)} %get-tuple-element.257), channel_id=1, source_target_pairs={{0,16},{8,24},{16,0},{24,8},{1,17},{9,25},{17,1},{25,9},{2,18},{10... | collective-permute-start | bytes 1007624 | tf_op jit(solution)/shard_map/ppermute | solution.py:701
  288.8 19.3 %collective-permute-start.25 = (bf16[656,256]{1,0:T(8,128)(2,1)}, bf16[656,256]{1,0:T(8,128)(2,1)S(1)}, u32[]{:S(2)}, u32[]{:S(2)}) collective-permute-start(bf16[656,256]{1,0:T(8,128)(2,1)} %get-tuple-element.258), channel_id=1, source_target_pairs={{0,24},{8,16},{16,8},{24,0},{1,25},{9,17},{17,9},{25,1},{2,26},{10... | collective-permute-start | bytes 1007624 | tf_op jit(solution)/shard_map/ppermute | solution.py:701
  309.4 20.4 %collective-permute-start.32 = (bf16[128,3072]{1,0:T(8,128)(2,1)S(1)}, bf16[128,3072]{1,0:T(8,128)(2,1)S(1)}, u32[]{:S(2)}, u32[]{:S(2)}) collective-permute-start(bf16[128,3072]{1,0:T(8,128)(2,1)S(1)} %pad_maximum_fusion.1.refs_1_), channel_id=1, source_target_pairs={{0,8},{8,0},{16,24},{24,16},{1,9},{9,1},{17,25},{25,17},{2,10},{10... | collective-permute-start | bytes 2359304 | tf_op jit(solution)/shard_map/ppermute | solution.py:701
  309.5 20.3 %collective-permute-start.33 = (bf16[128,3072]{1,0:T(8,128)(2,1)S(1)}, bf16[128,3072]{1,0:T(8,128)(2,1)S(1)}, u32[]{:S(2)}, u32[]{:S(2)}) collective-permute-start(bf16[128,3072]{1,0:T(8,128)(2,1)S(1)} %pad_maximum_fusion.1.refs_1_), channel_id=1, source_target_pairs={{0,16},{8,24},{16,0},{24,8},{1,17},{9,25},{17,1},{25,9},{2,18},{10... | collective-permute-start | bytes 2359304 | tf_op jit(solution)/shard_map/ppermute | solution.py:701
  315.0 12.3 %collective-permute-start.27 = (bf16[240,256]{1,0:T(8,128)(2,1)}, bf16[240,256]{1,0:T(8,128)(2,1)S(1)}, u32[]{:S(2)}, u32[]{:S(2)}) collective-permute-start(bf16[240,256]{1,0:T(8,128)(2,1)} %get-tuple-element.267), channel_id=1, source_target_pairs={{0,4},{2,6},{4,0},{6,2},{1,5},{3,7},{5,1},{7,3},{8,12},{10,14},{12... | collective-permute-start | bytes 368648 | tf_op jit(solution)/shard_map/ppermute | solution.py:704
  329.8 18.6 %collective-permute-start.37 = (bf16[128,1536]{1,0:T(8,128)(2,1)S(1)}, bf16[128,1536]{1,0:T(8,128)(2,1)S(1)}, u32[]{:S(2)}, u32[]{:S(2)}) collective-permute-start(bf16[128,1536]{1,0:T(8,128)(2,1)S(1)} %slice.22), channel_id=1, source_target_pairs={{0,16},{8,24},{16,0},{24,8},{1,17},{9,25},{17,1},{25,9},{2,18},{10... | collective-permute-start | bytes 1179656 | tf_op jit(solution)/shard_map/ppermute | solution.py:701
  330.8 17.7 %collective-permute-start.38 = (bf16[128,1536]{1,0:T(8,128)(2,1)S(1)}, bf16[128,1536]{1,0:T(8,128)(2,1)}, u32[]{:S(2)}, u32[]{:S(2)}) collective-permute-start(bf16[128,1536]{1,0:T(8,128)(2,1)S(1)} %slice.23), channel_id=1, source_target_pairs={{0,8},{8,0},{16,24},{24,16},{1,9},{9,1},{17,25},{25,17},{2,10},{10... | collective-permute-start | bytes 1179656 | tf_op jit(solution)/shard_map/ppermute | solution.py:701
  332.5 10.6 %collective-permute-start.34 = (bf16[224,256]{1,0:T(8,128)(2,1)}, bf16[224,256]{1,0:T(8,128)(2,1)}, u32[]{:S(2)}, u32[]{:S(2)}) collective-permute-start(bf16[224,256]{1,0:T(8,128)(2,1)} %get-tuple-element.272.refs_1_), channel_id=1, source_target_pairs={{0,8},{8,0},{16,24},{24,16},{1,9},{9,1},{17,25},{25,17},{2,10},{10... | collective-permute-start | bytes 344072 | tf_op jit(solution)/shard_map/ppermute | solution.py:701
  332.8 10.2 %collective-permute-start.35 = (bf16[224,256]{1,0:T(8,128)(2,1)}, bf16[224,256]{1,0:T(8,128)(2,1)}, u32[]{:S(2)}, u32[]{:S(2)}) collective-permute-start(bf16[224,256]{1,0:T(8,128)(2,1)} %get-tuple-element.272.refs_1_), channel_id=1, source_target_pairs={{0,16},{8,24},{16,0},{24,8},{1,17},{9,25},{17,1},{25,9},{2,18},{10... | collective-permute-start | bytes 344072 | tf_op jit(solution)/shard_map/ppermute | solution.py:701
  334.1 10.8 %collective-permute-start.36 = (bf16[224,256]{1,0:T(8,128)(2,1)}, bf16[224,256]{1,0:T(8,128)(2,1)}, u32[]{:S(2)}, u32[]{:S(2)}) collective-permute-start(bf16[224,256]{1,0:T(8,128)(2,1)} %get-tuple-element.272.refs_1_), channel_id=1, source_target_pairs={{0,24},{8,16},{16,8},{24,0},{1,25},{9,17},{17,9},{25,1},{2,26},{10... | collective-permute-start | bytes 344072 | tf_op jit(solution)/shard_map/ppermute | solution.py:701
  (49 other events, 387.3 us)
Sparse Core Ops, SparseCore 0:
  161.7 77.1 reduce-scatter.2
  259.1 44.0 reduce-scatter.4
